TPU v7x, 512 devices: a whole 4x8x8 slice. The times are simulated.
512 devices in a mesh: node: 8 (over z), local: 64 (over x, y, core).
Axes of the slice: x: 4, y: 8, z: 8, core: 2. Of those that a mesh axis runs over, the one named last changes fastest.
Arguments:
- tokens: bfloat16 [4096, 7168], P('node', 'local'), may hold values from -6 to 6
- out_grad: bfloat16 [4096, 7168], P('node', 'local'), may hold values from -1.1953125 to 1.1953125
- route_ids: int32 [4096, 8], P('node'), may hold values from 0 to 255, as said below
- route_weights: float32 [4096, 8], P('node'), may hold values from 0.2 to 1
- gate_weight: bfloat16 [8, 64, 896, 256], P('node', 'local'), may hold values from -0.0625 to 0.0625
- up_weight: bfloat16 [8, 64, 896, 256], P('node', 'local'), may hold values from -0.0625 to 0.0625
- down_weight: bfloat16 [8, 64, 256, 896], P('node', 'local'), may hold values from -0.125 to 0.125
Outputs:
- layer_out: bfloat16 [4096, 7168], P('node', 'local')
- input_grad: bfloat16 [4096, 7168], P('node', 'local')
- gate_grad: bfloat16 [8, 64, 896, 256], P('node', 'local')
- up_grad: bfloat16 [8, 64, 896, 256], P('node', 'local')
- down_grad: bfloat16 [8, 64, 256, 896], P('node', 'local')
Inputs may be any that keep to these rules, and one draw needn't show every extreme that they name: `route_ids`: each row names 8 different experts, all from 4 of the 8 blocks of 32 consecutive numbers. Call the multiples of 32 the computed experts. A row names at most one computed expert. Within each node group's 512 consecutive rows, each computed expert is named by at most 32 rows, and in every draw some computed expert is named by exactly 32 rows of every node group's rows.
All inputs are finite; a program needn't handle non-finite values.
Results may differ from a plain program's by a relative error of at most 0.0058.
Values may be sent and summed in bfloat16 or wider, within the bound.
A program may use at most 64 MiB of HBM per device.

v0:
```python
import jax
import jax.numpy as jnp
from jax import lax
from jax.sharding import PartitionSpec as P

EXPERTS = 256
CAP = 32


def from_partner(block, axis, bit):
    count = lax.axis_size(axis)
    route = []
    for low in range(count):
        high = low | 1 << bit
        if high != low and high < count:
            route += [(low, high), (high, low)]
    return lax.ppermute(block, axis, route)


def gather_bits(portion, lane_index, bit_list, axis_dim, trader):
    for bit_pos in bit_list:
        partner = trader(portion, bit_pos)
        upper_side = lane_index >> bit_pos & 1 == 1
        portion = jnp.where(
            upper_side,
            jnp.concatenate([partner, portion], axis_dim),
            jnp.concatenate([portion, partner], axis_dim),
        )
    return portion


def halve_bits(portion, lane_index, bit_list, axis_dim, trader):
    for bit_pos in bit_list:
        middle = portion.shape[axis_dim] // 2
        low_half = lax.slice_in_dim(portion, 0, middle, axis=axis_dim)
        high_half = lax.slice_in_dim(portion, middle, 2 * middle, axis=axis_dim)
        upper_side = lane_index >> bit_pos & 1 == 1
        kept_half = jnp.where(upper_side, high_half, low_half)
        sent_half = jnp.where(upper_side, low_half, high_half)
        portion = kept_half + trader(sent_half, bit_pos)
    return portion


def contract(left_side, right_side, left_dim, right_dim):
    return lax.dot_general(
        left_side,
        right_side,
        (((left_dim,), (right_dim,)), ((), ())),
        preferred_element_type=jnp.float32,
    )


def route_slots(route_ids, route_weights, groups, capacity):
    owned_ids = jnp.arange(groups, dtype=jnp.int32) * (EXPERTS // groups)
    matches = route_ids[:, :, None] == owned_ids[None, None, :]
    hit_mask = jnp.any(matches, axis=1)
    hit_weight = jnp.sum(jnp.where(matches, route_weights[:, :, None], 0.0), axis=1)
    rank_in = jnp.cumsum(hit_mask.astype(jnp.int32), axis=0) - 1
    count_rows = route_ids.shape[0]
    target = jnp.where(
        hit_mask,
        jnp.arange(groups, dtype=jnp.int32)[None, :] * capacity + rank_in,
        groups * capacity,
    )
    flat_target = target.reshape(-1)
    token_number = jnp.broadcast_to(
        jnp.arange(count_rows, dtype=jnp.int32)[:, None], target.shape
    ).reshape(-1)
    slot_token = (
        jnp.zeros((groups * capacity,), jnp.int32).at[flat_target].set(token_number, mode="drop")
    )
    slot_weight = (
        jnp.zeros((groups * capacity,), jnp.float32)
        .at[flat_target]
        .set(hit_weight.reshape(-1), mode="drop")
    )
    slot_live = jnp.zeros((groups * capacity,), jnp.bool_).at[flat_target].set(True, mode="drop")
    return (target, hit_mask, hit_weight, slot_token, slot_weight, slot_live)


def on_device(tokens, out_grad, route_ids, route_weights, gate_weight, up_weight, down_weight):
    groups = lax.axis_size("node")
    lane_index = lax.axis_index("local")
    feature_parts = lax.axis_size("local") // 8
    part_bits = list(range(3, 3 + feature_parts.bit_length() - 1))
    unit_bits = [0, 1, 2]
    capacity = CAP
    width_local = tokens.shape[1]
    total_rows = groups * capacity
    target, hit_mask, hit_weight, slot_token, slot_weight, slot_live = route_slots(
        route_ids, route_weights, groups, capacity
    )
    sent_tokens = jnp.where(slot_live[:, None], tokens[slot_token], jnp.zeros((), tokens.dtype))
    sent_grads = (slot_weight[:, None] * out_grad[slot_token].astype(jnp.float32)).astype(
        jnp.bfloat16
    )
    outgoing = jnp.stack([sent_tokens, sent_grads]).reshape(2, groups, capacity, width_local)
    landed = lax.all_to_all(outgoing, "node", split_axis=1, concat_axis=1, tiled=True).reshape(
        2, total_rows, width_local
    )
    arrived = gather_bits(
        landed,
        lane_index,
        unit_bits,
        2,
        lambda portion, bit_pos: from_partner(portion, "local", bit_pos),
    )
    expert_in = arrived[0]
    expert_grad = arrived[1]
    w_gate = gate_weight[0, 0]
    w_up = up_weight[0, 0]
    w_down = down_weight[0, 0]
    partial_terms = jnp.stack(
        [
            jnp.dot(expert_in, w_gate, preferred_element_type=jnp.float32),
            jnp.dot(expert_in, w_up, preferred_element_type=jnp.float32),
        ]
    )
    back_part = contract(expert_grad, w_down, 1, 1)
    shares = halve_bits(
        partial_terms,
        lane_index,
        part_bits[::-1],
        1,
        lambda portion, bit_pos: from_partner(portion, "local", bit_pos),
    )
    gate_sum = shares[0]
    up_sum = shares[1]
    sigmoid_gate = jax.nn.sigmoid(gate_sum)
    active = gate_sum * sigmoid_gate
    hidden_share = (active * up_sum).astype(jnp.bfloat16)
    hidden = gather_bits(
        hidden_share,
        lane_index,
        part_bits,
        0,
        lambda portion, bit_pos: from_partner(portion, "local", bit_pos),
    )
    back_share = halve_bits(
        back_part,
        lane_index,
        part_bits[::-1],
        0,
        lambda portion, bit_pos: from_partner(portion, "local", bit_pos),
    )
    gate_share = (
        back_share * up_sum * sigmoid_gate * (1.0 + gate_sum * (1.0 - sigmoid_gate))
    ).astype(jnp.bfloat16)
    up_share = (back_share * active).astype(jnp.bfloat16)
    grad_pair = gather_bits(
        jnp.stack([gate_share, up_share]),
        lane_index,
        part_bits,
        1,
        lambda portion, bit_pos: from_partner(portion, "local", bit_pos),
    )
    grad_gate = grad_pair[0]
    grad_up = grad_pair[1]
    out_part = jnp.dot(hidden, w_down, preferred_element_type=jnp.float32)
    in_part = contract(grad_gate, w_gate, 1, 1) + contract(grad_up, w_up, 1, 1)
    gate_grad = contract(expert_in, grad_gate, 0, 0).astype(jnp.bfloat16)[None, None]
    up_grad = contract(expert_in, grad_up, 0, 0).astype(jnp.bfloat16)[None, None]
    down_grad = contract(hidden, expert_grad, 0, 0).astype(jnp.bfloat16)[None, None]
    partials = jnp.stack([out_part, in_part])
    reduced = halve_bits(
        partials,
        lane_index,
        unit_bits[::-1],
        2,
        lambda portion, bit_pos: from_partner(portion, "local", bit_pos),
    ).astype(jnp.bfloat16)
    returned = lax.all_to_all(
        reduced.reshape(2, groups, capacity, width_local),
        "node",
        split_axis=1,
        concat_axis=1,
        tiled=True,
    )
    flat_back = returned.reshape(2, total_rows, width_local)
    safe_target = jnp.minimum(target, total_rows - 1)
    picked = flat_back[:, safe_target]
    layer_out = jnp.sum(hit_weight[:, :, None] * picked[0].astype(jnp.float32), axis=1).astype(
        jnp.bfloat16
    )
    input_grad = jnp.sum(
        jnp.where(hit_mask[:, :, None], picked[1].astype(jnp.float32), 0.0), axis=1
    ).astype(jnp.bfloat16)
    return (layer_out, input_grad, gate_grad, up_grad, down_grad)


def solution(mesh):
    placed = (
        P("node", "local"),
        P("node", "local"),
        P("node", None),
        P("node", None),
        P("node", "local", None, None),
        P("node", "local", None, None),
        P("node", "local", None, None),
    )
    return jax.shard_map(
        on_device,
        mesh=mesh,
        in_specs=placed,
        out_specs=(
            P("node", "local"),
            P("node", "local"),
            P("node", "local", None, None),
            P("node", "local", None, None),
            P("node", "local", None, None),
        ),
        check_vma=False,
    )
```

profile of v0, /device:TPU:1, one launch (start us, length us, event | category | flops | bytes accessed | tf_op | source)
XLA Modules:
  0.0 287.7 jit_solution(13383460139030167692)
XLA Ops:
  4.6 15.5 %scatter_custom_fusion.1 = s32[256]{0:T(256)S(1)} fusion(s32[4096]{0:T(1024)S(1)} %bitcast.117, s32[4096]{0:T(1024)S(1)} %reshape.185, s32[]{:T(128)} %constant.20.clone.1), kind=kCustom, calls=%fused_computation.101 | custom fusion | bytes 1028 | tf_op jit(solution)/shard_map/scatter | solution.py:70
  21.3 15.5 %scatter_custom_fusion.2 = f32[256]{0:T(256)S(1)} fusion(s32[4096]{0:T(1024)S(1)} %bitcast.118, f32[4096]{0:T(1024)S(1)} %reshape.193, f32[]{:T(128)} %constant.18.clone.1), kind=kCustom, calls=%fused_computation.99 | custom fusion | bytes 1028 | tf_op jit(solution)/shard_map/scatter | solution.py:75
  38.7 17.6 %scatter_custom_fusion = pred[256]{0:T(512)(128)(4,1)S(1)} fusion(s32[4096]{0:T(1024)S(1)} %bitcast.119, pred[4096]{0:T(1024)(128)(4,1)S(1)} %broadcast.92, pred[]{:T(512)} %constant.26.clone.1), kind=kCustom, calls=%fused_computation.97 | custom fusion | bytes 257 | tf_op jit(solution)/shard_map/scatter | solution.py:77
  56.7 18.6 %all_to_all.10 = bf16[2,8,32,112]{3,2,0,1:T(8,128)(2,1)S(1)} all-to-all(bf16[2,8,32,112]{3,2,0,1:T(8,128)(2,1)S(1)} %pad_maximum_fusion.2), channel_id=1, replica_groups=mesh['node'=8,'local'=64] {'node'}, dimensions={1} | all-to-all | bytes 229376 | tf_op jit(solution)/shard_map/all_to_all | solution.py:98
  75.2 4.2 %collective-permute-start = (bf16[2,256,112]{2,1,0:T(8,128)(2,1)S(1)}, bf16[2,256,112]{2,1,0:T(8,128)(2,1)S(1)}, u32[]{:S(2)}, u32[]{:S(2)}) collective-permute-start(bf16[2,256,112]{2,1,0:T(8,128)(2,1)S(1)} %bitcast.112), channel_id=1, source_target_pairs={{0,1},{1,0},{2,3},{3,2},{4,5},{5,4},{6,7},{7,6},{8,9},{9,8},{10,11... | collective-permute-start | bytes 344072 | tf_op jit(solution)/shard_map/ppermute | solution.py:17
  80.7 3.2 %collective-permute-start.1 = (bf16[2,256,224]{2,1,0:T(8,128)(2,1)S(1)}, bf16[2,256,224]{2,1,0:T(8,128)(2,1)S(1)}, u32[]{:S(2)}, u32[]{:S(2)}) collective-permute-start(bf16[2,256,224]{2,1,0:T(8,128)(2,1)S(1)} %maximum_select_fusion.2), channel_id=1, source_target_pairs={{0,2},{2,0},{1,3},{3,1},{4,6},{6,4},{5,7},{7,5},{8,10},{10,8},{9,1... | collective-permute-start | bytes 688136 | tf_op jit(solution)/shard_map/ppermute | solution.py:17
  83.9 6.2 %collective-permute-done.1 = bf16[2,256,224]{2,1,0:T(8,128)(2,1)S(1)} collective-permute-done((bf16[2,256,224]{2,1,0:T(8,128)(2,1)S(1)}, bf16[2,256,224]{2,1,0:T(8,128)(2,1)S(1)}, u32[]{:S(2)}, u32[]{:S(2)}) %collective-permute-start.1) | collective-permute-done | bytes 229408 | tf_op jit(solution)/shard_map/ppermute | solution.py:17
  90.5 4.2 %collective-permute-start.2 = (bf16[2,256,448]{2,1,0:T(8,128)(2,1)S(1)}, bf16[2,256,448]{2,1,0:T(8,128)(2,1)S(1)}, u32[]{:S(2)}, u32[]{:S(2)}) collective-permute-start(bf16[2,256,448]{2,1,0:T(8,128)(2,1)S(1)} %maximum_select_fusion.1), channel_id=1, source_target_pairs={{0,4},{4,0},{1,5},{5,1},{2,6},{6,2},{3,7},{7,3},{8,12},{12,8},{9,1... | collective-permute-start | bytes 1376264 | tf_op jit(solution)/shard_map/ppermute | solution.py:17
  94.7 22.5 %collective-permute-done.2 = bf16[2,256,448]{2,1,0:T(8,128)(2,1)S(1)} collective-permute-done((bf16[2,256,448]{2,1,0:T(8,128)(2,1)S(1)}, bf16[2,256,448]{2,1,0:T(8,128)(2,1)S(1)}, u32[]{:S(2)}, u32[]{:S(2)}) %collective-permute-start.2) | collective-permute-done | bytes 458784 | tf_op jit(solution)/shard_map/ppermute | solution.py:17
  118.6 4.7 %collective-permute-start.9 = (f32[128,256]{1,0:T(8,128)S(1)}, f32[128,256]{1,0:T(8,128)S(1)}, u32[]{:S(2)}, u32[]{:S(2)}) collective-permute-start(f32[128,256]{1,0:T(8,128)S(1)} %slice_select_fusion.2), channel_id=1, source_target_pairs={{0,32},{32,0},{1,33},{33,1},{2,34},{34,2},{3,35},{35,3},{4,36},{36... | collective-permute-start | bytes 393224 | tf_op jit(solution)/shard_map/ppermute | solution.py:17
  123.6 2.1 collective-permute-start.3
  125.8 3.1 %collective-permute-start.10 = (f32[64,256]{1,0:T(8,128)S(1)}, f32[64,256]{1,0:T(8,128)S(1)}, u32[]{:S(2)}, u32[]{:S(2)}) collective-permute-start(f32[64,256]{1,0:T(8,128)S(1)} %slice_select_fusion.4), channel_id=1, source_target_pairs={{0,16},{16,0},{1,17},{17,1},{2,18},{18,2},{3,19},{19,3},{4,20},{20... | collective-permute-start | bytes 196616 | tf_op jit(solution)/shard_map/ppermute | solution.py:17
  129.0 4.0 %collective-permute-done.3 = f32[2,128,256]{2,1,0:T(8,128)S(1)} collective-permute-done((f32[2,128,256]{2,1,0:T(8,128)S(1)}, f32[2,128,256]{2,1,0:T(8,128)S(1)}, u32[]{:S(2)}, u32[]{:S(2)}) %collective-permute-start.3) | collective-permute-done | bytes 262176 | tf_op jit(solution)/shard_map/ppermute | solution.py:17
  133.0 2.2 collective-permute-start.4
  135.3 3.5 %collective-permute-done.4 = f32[2,64,256]{2,1,0:T(8,128)S(1)} collective-permute-done((f32[2,64,256]{2,1,0:T(8,128)S(1)}, f32[2,64,256]{2,1,0:T(8,128)S(1)}, u32[]{:S(2)}, u32[]{:S(2)}) %collective-permute-start.4) | collective-permute-done | bytes 131104 | tf_op jit(solution)/shard_map/ppermute | solution.py:17
  138.8 9.4 %collective-permute-start.5 = (f32[2,32,256]{2,1,0:T(8,128)S(1)}, f32[2,32,256]{2,1,0:T(8,128)S(1)}, u32[]{:S(2)}, u32[]{:S(2)}) collective-permute-start(f32[2,32,256]{2,1,0:T(8,128)S(1)} %slice_select_fusion.5), channel_id=1, source_target_pairs={{0,8},{8,0},{1,9},{9,1},{2,10},{10,2},{3,11},{11,3},{4,12},{12,4},... | collective-permute-start | bytes 196616 | tf_op jit(solution)/shard_map/ppermute | solution.py:17
  150.2 6.6 %collective-permute-done.11 = f32[32,256]{1,0:T(8,128)S(1)} collective-permute-done((f32[32,256]{1,0:T(8,128)S(1)}, f32[32,256]{1,0:T(8,128)S(1)}, u32[]{:S(2)}, u32[]{:S(2)}) %collective-permute-start.11) | collective-permute-done | bytes 32800 | tf_op jit(solution)/shard_map/ppermute | solution.py:17
  158.8 7.4 %collective-permute-start.12 = (bf16[2,32,256]{2,1,0:T(8,128)(2,1)S(1)}, bf16[2,32,256]{2,1,0:T(8,128)(2,1)S(1)}, u32[]{:S(2)}, u32[]{:S(2)}) collective-permute-start(bf16[2,32,256]{2,1,0:T(8,128)(2,1)S(1)} %pad_maximum_fusion.3), channel_id=1, source_target_pairs={{0,8},{8,0},{1,9},{9,1},{2,10},{10,2},{3,11},{11,3},{4,12},{12,4},... | collective-permute-start | bytes 98312 | tf_op jit(solution)/shard_map/ppermute | solution.py:17
  166.2 2.2 collective-permute-start.7
  168.5 3.1 %collective-permute-start.13 = (bf16[2,64,256]{2,1,0:T(8,128)(2,1)S(1)}, bf16[2,64,256]{2,1,0:T(8,128)(2,1)S(1)}, u32[]{:S(2)}, u32[]{:S(2)}) collective-permute-start(bf16[2,64,256]{2,1,0:T(8,128)(2,1)S(1)} %maximum_select_fusion.7), channel_id=1, source_target_pairs={{0,16},{16,0},{1,17},{17,1},{2,18},{18,2},{3,19},{19,3},{4,20},{20... | collective-permute-start | bytes 196616 | tf_op jit(solution)/shard_map/ppermute | solution.py:17
  171.6 2.9 %collective-permute-start.8 = (bf16[128,256]{1,0:T(8,128)(2,1)S(1)}, bf16[128,256]{1,0:T(8,128)(2,1)S(1)}, u32[]{:S(2)}, u32[]{:S(2)}) collective-permute-start(bf16[128,256]{1,0:T(8,128)(2,1)S(1)} %maximum_select_fusion.6), channel_id=1, source_target_pairs={{0,32},{32,0},{1,33},{33,1},{2,34},{34,2},{3,35},{35,3},{4,36},{36... | collective-permute-start | bytes 196616 | tf_op jit(solution)/shard_map/ppermute | solution.py:17
  174.6 4.1 %collective-permute-start.14 = (bf16[2,128,256]{2,1,0:T(8,128)(2,1)S(1)}, bf16[2,128,256]{2,1,0:T(8,128)(2,1)S(1)}, u32[]{:S(2)}, u32[]{:S(2)}) collective-permute-start(bf16[2,128,256]{2,1,0:T(8,128)(2,1)S(1)} %maximum_select_fusion.5), channel_id=1, source_target_pairs={{0,32},{32,0},{1,33},{33,1},{2,34},{34,2},{3,35},{35,3},{4,36},{36... | collective-permute-start | bytes 393224 | tf_op jit(solution)/shard_map/ppermute | solution.py:17
  179.0 2.8 collective-permute-done.14
  186.4 42.1 %collective-permute-done.15 = f32[2,256,448]{1,2,0:T(8,128)S(1)} collective-permute-done((f32[2,256,448]{1,2,0:T(8,128)}, f32[2,256,448]{1,2,0:T(8,128)S(1)}, u32[]{:S(2)}, u32[]{:S(2)}) %collective-permute-start.15) | collective-permute-done | bytes 917536 | tf_op jit(solution)/shard_map/ppermute | solution.py:17
  232.4 2.0 collective-permute-start.16
  234.8 11.9 %collective-permute-done.16 = f32[2,256,224]{2,1,0:T(8,128)S(1)} collective-permute-done((f32[2,256,224]{2,1,0:T(8,128)}, f32[2,256,224]{2,1,0:T(8,128)S(1)}, u32[]{:S(2)}, u32[]{:S(2)}) %collective-permute-start.16) | collective-permute-done | bytes 458784 | tf_op jit(solution)/shard_map/ppermute | solution.py:17
  247.1 4.2 %collective-permute-start.17 = (f32[2,256,112]{2,1,0:T(8,128)S(1)}, f32[2,256,112]{2,1,0:T(8,128)S(1)}, u32[]{:S(2)}, u32[]{:S(2)}) collective-permute-start(f32[2,256,112]{2,1,0:T(8,128)S(1)} %slice_select_fusion.1), channel_id=1, source_target_pairs={{0,1},{1,0},{2,3},{3,2},{4,5},{5,4},{6,7},{7,6},{8,9},{9,8},{10,11... | collective-permute-start | bytes 688136 | tf_op jit(solution)/shard_map/ppermute | solution.py:17
  252.8 2.0 fusion.5
  255.6 3.4 %all-to-all-start.1 = ((bf16[2,8,32,112]{3,2,0,1:T(8,128)(2,1)}), bf16[2,8,32,112]{3,2,0,1:T(8,128)(2,1)S(1)}, u32[]{:S(2)}, u32[]{:S(2)}) async-start(bf16[2,8,32,112]{3,2,0,1:T(8,128)(2,1)} %copy.67), calls=%async_computation.1 | async-start | bytes 262144 | tf_op jit(solution)/shard_map/all_to_all | solution.py:172
  261.2 7.2 %all-to-all-done.1 = bf16[2,8,32,112]{3,2,0,1:T(8,128)(2,1)S(1)} async-done(((bf16[2,8,32,112]{3,2,0,1:T(8,128)(2,1)}), bf16[2,8,32,112]{3,2,0,1:T(8,128)(2,1)S(1)}, u32[]{:S(2)}, u32[]{:S(2)}) %all-to-all-start.1) | async-done | bytes 114720 | tf_op jit(solution)/shard_map/all_to_all | solution.py:172
  268.4 13.7 %gather_fusion.2 = bf16[4096,2,112]{2,1,0:T(2,128)(2,1)S(1)} fusion(bf16[2,256,112]{2,0,1:T(2,128)(2,1)S(1)} %bitcast.109, s32[4096]{0:T(1024)S(1)} %broadcast_clamp_fusion), kind=kCustom, calls=%fused_computation.2 | custom fusion | bytes 3686400 | tf_op jit(solution)/shard_map/gather | solution.py:181
  283.1 3.1 %fusion = (bf16[512,112]{1,0:T(8,128)(2,1)S(1)}, bf16[512,112]{1,0:T(8,128)(2,1)S(1)}) fusion(bf16[2,512,8,112]{3,2,1,0:T(8,128)(2,1)S(1)} %bitcast.110, pred[512,8]{1,0:T(8,128)(4,1)S(1)} %copy-done.10, f32[512,8]{1,0:T(8,128)S(1)} %copy-done.4), kind=kLoop, calls=%fused_computation.7 | loop fusion | flops 2637824 | bytes 2084864 | tf_op jit(solution)/shard_map/reduce_sum | solution.py:185
  (117 shorter events, 31.1 us)
Async XLA Ops:
  0.6 117.6 %copy-start = (bf16[1,1,256,896]{3,2,1,0:T(8,128)(2,1)S(1)}, bf16[1,1,256,896]{3,2,1,0:T(8,128)(2,1)}, u32[]{:S(2)}) copy-start(bf16[1,1,256,896]{3,2,1,0:T(8,128)(2,1)} %param.13) | copy-start | bytes 1376260
  0.6 36.2 %copy-start.11 = (bf16[512,112]{0,1:T(8,128)(2,1)S(1)}, bf16[512,112]{0,1:T(8,128)(2,1)}, u32[]{:S(2)}) copy-start(bf16[512,112]{0,1:T(8,128)(2,1)} %param.7) | copy-start | bytes 344068
  2.6 1.5 copy-start.13
  21.1 15.7 %copy-start.3 = (f32[512,8]{1,0:T(8,128)}, f32[512,8]{1,0:T(8,128)S(1)}, u32[]{:S(2)}) copy-start(f32[512,8]{1,0:T(8,128)S(1)} %copy.57) | copy-start | bytes 49156
  56.7 61.2 %copy-start.5 = (bf16[1,1,896,256]{3,2,1,0:T(8,128)(2,1)S(1)}, bf16[1,1,896,256]{3,2,1,0:T(8,128)(2,1)}, u32[]{:S(2)}) copy-start(bf16[1,1,896,256]{3,2,1,0:T(8,128)(2,1)} %param.12) | copy-start | bytes 1376260
  75.2 5.2 %collective-permute-start = (bf16[2,256,112]{2,1,0:T(8,128)(2,1)S(1)}, bf16[2,256,112]{2,1,0:T(8,128)(2,1)S(1)}, u32[]{:S(2)}, u32[]{:S(2)}) collective-permute-start(bf16[2,256,112]{2,1,0:T(8,128)(2,1)S(1)} %bitcast.112), channel_id=1, source_target_pairs={{0,1},{1,0},{2,3},{3,2},{4,5},{5,4},{6,7},{7,6},{8,9},{9,8},{10,11... | collective-permute-start | bytes 344072 | tf_op jit(solution)/shard_map/ppermute | solution.py:17
  80.7 9.4 %collective-permute-start.1 = (bf16[2,256,224]{2,1,0:T(8,128)(2,1)S(1)}, bf16[2,256,224]{2,1,0:T(8,128)(2,1)S(1)}, u32[]{:S(2)}, u32[]{:S(2)}) collective-permute-start(bf16[2,256,224]{2,1,0:T(8,128)(2,1)S(1)} %maximum_select_fusion.2), channel_id=1, source_target_pairs={{0,2},{2,0},{1,3},{3,1},{4,6},{6,4},{5,7},{7,5},{8,10},{10,8},{9,1... | collective-permute-start | bytes 688136 | tf_op jit(solution)/shard_map/ppermute | solution.py:17
  90.5 26.8 %collective-permute-start.2 = (bf16[2,256,448]{2,1,0:T(8,128)(2,1)S(1)}, bf16[2,256,448]{2,1,0:T(8,128)(2,1)S(1)}, u32[]{:S(2)}, u32[]{:S(2)}) collective-permute-start(bf16[2,256,448]{2,1,0:T(8,128)(2,1)S(1)} %maximum_select_fusion.1), channel_id=1, source_target_pairs={{0,4},{4,0},{1,5},{5,1},{2,6},{6,2},{3,7},{7,3},{8,12},{12,8},{9,1... | collective-permute-start | bytes 1376264 | tf_op jit(solution)/shard_map/ppermute | solution.py:17
  94.7 28.5 %copy-start.7 = (bf16[1,1,896,256]{3,2,1,0:T(8,128)(2,1)S(1)}, bf16[1,1,896,256]{3,2,1,0:T(8,128)(2,1)}, u32[]{:S(2)}) copy-start(bf16[1,1,896,256]{3,2,1,0:T(8,128)(2,1)} %param.11) | copy-start | bytes 1376260
  117.9 5.7 %copy-start.1 = (bf16[2,256,896]{2,1,0:T(8,128)(2,1)}, bf16[2,256,896]{2,1,0:T(8,128)(2,1)S(1)}, u32[]{:S(2)}) copy-start(bf16[2,256,896]{2,1,0:T(8,128)(2,1)S(1)} %maximum_select_fusion) | copy-start | bytes 2752516
  118.6 7.2 %collective-permute-start.9 = (f32[128,256]{1,0:T(8,128)S(1)}, f32[128,256]{1,0:T(8,128)S(1)}, u32[]{:S(2)}, u32[]{:S(2)}) collective-permute-start(f32[128,256]{1,0:T(8,128)S(1)} %slice_select_fusion.2), channel_id=1, source_target_pairs={{0,32},{32,0},{1,33},{33,1},{2,34},{34,2},{3,35},{35,3},{4,36},{36... | collective-permute-start | bytes 393224 | tf_op jit(solution)/shard_map/ppermute | solution.py:17
  123.6 9.3 %collective-permute-start.3 = (f32[2,128,256]{2,1,0:T(8,128)S(1)}, f32[2,128,256]{2,1,0:T(8,128)S(1)}, u32[]{:S(2)}, u32[]{:S(2)}) collective-permute-start(f32[2,128,256]{2,1,0:T(8,128)S(1)} %broadcast_select_fusion.1), channel_id=1, source_target_pairs={{0,32},{32,0},{1,33},{33,1},{2,34},{34,2},{3,35},{35,3},{4,36},{36... | collective-permute-start | bytes 786440 | tf_op jit(solution)/shard_map/ppermute | solution.py:17
  125.8 9.4 %collective-permute-start.10 = (f32[64,256]{1,0:T(8,128)S(1)}, f32[64,256]{1,0:T(8,128)S(1)}, u32[]{:S(2)}, u32[]{:S(2)}) collective-permute-start(f32[64,256]{1,0:T(8,128)S(1)} %slice_select_fusion.4), channel_id=1, source_target_pairs={{0,16},{16,0},{1,17},{17,1},{2,18},{18,2},{3,19},{19,3},{4,20},{20... | collective-permute-start | bytes 196616 | tf_op jit(solution)/shard_map/ppermute | solution.py:17
  133.0 5.7 %collective-permute-start.4 = (f32[2,64,256]{2,1,0:T(8,128)S(1)}, f32[2,64,256]{2,1,0:T(8,128)S(1)}, u32[]{:S(2)}, u32[]{:S(2)}) collective-permute-start(f32[2,64,256]{2,1,0:T(8,128)S(1)} %slice_select_fusion.3), channel_id=1, source_target_pairs={{0,16},{16,0},{1,17},{17,1},{2,18},{18,2},{3,19},{19,3},{4,20},{20... | collective-permute-start | bytes 393224 | tf_op jit(solution)/shard_map/ppermute | solution.py:17
  138.8 11.4 %collective-permute-start.5 = (f32[2,32,256]{2,1,0:T(8,128)S(1)}, f32[2,32,256]{2,1,0:T(8,128)S(1)}, u32[]{:S(2)}, u32[]{:S(2)}) collective-permute-start(f32[2,32,256]{2,1,0:T(8,128)S(1)} %slice_select_fusion.5), channel_id=1, source_target_pairs={{0,8},{8,0},{1,9},{9,1},{2,10},{10,2},{3,11},{11,3},{4,12},{12,4},... | collective-permute-start | bytes 196616 | tf_op jit(solution)/shard_map/ppermute | solution.py:17
  148.2 8.6 %collective-permute-start.11 = (f32[32,256]{1,0:T(8,128)S(1)}, f32[32,256]{1,0:T(8,128)S(1)}, u32[]{:S(2)}, u32[]{:S(2)}) collective-permute-start(f32[32,256]{1,0:T(8,128)S(1)} %slice_select_fusion.6), channel_id=1, source_target_pairs={{0,8},{8,0},{1,9},{9,1},{2,10},{10,2},{3,11},{11,3},{4,12},{12,4},... | collective-permute-start | bytes 98312 | tf_op jit(solution)/shard_map/ppermute | solution.py:17
  156.8 9.4 %collective-permute-start.6 = (bf16[32,256]{1,0:T(8,128)(2,1)S(1)}, bf16[32,256]{1,0:T(8,128)(2,1)S(1)}, u32[]{:S(2)}, u32[]{:S(2)}) collective-permute-start(bf16[32,256]{1,0:T(8,128)(2,1)S(1)} %get-tuple-element.26), channel_id=1, source_target_pairs={{0,8},{8,0},{1,9},{9,1},{2,10},{10,2},{3,11},{11,3},{4,12},{12,4},... | collective-permute-start | bytes 49160 | tf_op jit(solution)/shard_map/ppermute | solution.py:17
  158.8 23.8 %copy-start.6 = (bf16[1,1,896,256]{3,2,1,0:T(8,128)(2,1)S(1)}, bf16[1,1,896,256]{3,2,1,0:T(8,128)(2,1)}, u32[]{:S(2)}) copy-start(bf16[1,1,896,256]{3,2,1,0:T(8,128)(2,1)} %param.12) | copy-start | bytes 1376260
  158.8 9.6 %collective-permute-start.12 = (bf16[2,32,256]{2,1,0:T(8,128)(2,1)S(1)}, bf16[2,32,256]{2,1,0:T(8,128)(2,1)S(1)}, u32[]{:S(2)}, u32[]{:S(2)}) collective-permute-start(bf16[2,32,256]{2,1,0:T(8,128)(2,1)S(1)} %pad_maximum_fusion.3), channel_id=1, source_target_pairs={{0,8},{8,0},{1,9},{9,1},{2,10},{10,2},{3,11},{11,3},{4,12},{12,4},... | collective-permute-start | bytes 98312 | tf_op jit(solution)/shard_map/ppermute | solution.py:17
  166.2 5.3 %collective-permute-start.7 = (bf16[64,256]{1,0:T(8,128)(2,1)S(1)}, bf16[64,256]{1,0:T(8,128)(2,1)S(1)}, u32[]{:S(2)}, u32[]{:S(2)}) collective-permute-start(bf16[64,256]{1,0:T(8,128)(2,1)S(1)} %maximum_select_fusion.8), channel_id=1, source_target_pairs={{0,16},{16,0},{1,17},{17,1},{2,18},{18,2},{3,19},{19,3},{4,20},{20... | collective-permute-start | bytes 98312 | tf_op jit(solution)/shard_map/ppermute | solution.py:17
  168.5 6.0 %collective-permute-start.13 = (bf16[2,64,256]{2,1,0:T(8,128)(2,1)S(1)}, bf16[2,64,256]{2,1,0:T(8,128)(2,1)S(1)}, u32[]{:S(2)}, u32[]{:S(2)}) collective-permute-start(bf16[2,64,256]{2,1,0:T(8,128)(2,1)S(1)} %maximum_select_fusion.7), channel_id=1, source_target_pairs={{0,16},{16,0},{1,17},{17,1},{2,18},{18,2},{3,19},{19,3},{4,20},{20... | collective-permute-start | bytes 196616 | tf_op jit(solution)/shard_map/ppermute | solution.py:17
  171.6 7.0 %collective-permute-start.8 = (bf16[128,256]{1,0:T(8,128)(2,1)S(1)}, bf16[128,256]{1,0:T(8,128)(2,1)S(1)}, u32[]{:S(2)}, u32[]{:S(2)}) collective-permute-start(bf16[128,256]{1,0:T(8,128)(2,1)S(1)} %maximum_select_fusion.6), channel_id=1, source_target_pairs={{0,32},{32,0},{1,33},{33,1},{2,34},{34,2},{3,35},{35,3},{4,36},{36... | collective-permute-start | bytes 196616 | tf_op jit(solution)/shard_map/ppermute | solution.py:17
  174.6 7.2 %collective-permute-start.14 = (bf16[2,128,256]{2,1,0:T(8,128)(2,1)S(1)}, bf16[2,128,256]{2,1,0:T(8,128)(2,1)S(1)}, u32[]{:S(2)}, u32[]{:S(2)}) collective-permute-start(bf16[2,128,256]{2,1,0:T(8,128)(2,1)S(1)} %maximum_select_fusion.5), channel_id=1, source_target_pairs={{0,32},{32,0},{1,33},{33,1},{2,34},{34,2},{3,35},{35,3},{4,36},{36... | collective-permute-start | bytes 393224 | tf_op jit(solution)/shard_map/ppermute | solution.py:17
  178.6 3.2 %copy-start.12 = (bf16[128,256]{1,0:T(8,128)(2,1)}, bf16[128,256]{1,0:T(8,128)(2,1)S(1)}, u32[]{:S(2)}) copy-start(bf16[128,256]{1,0:T(8,128)(2,1)S(1)} %collective-permute-done.8) | copy-start | bytes 196612
  184.5 44.1 %collective-permute-start.15 = (f32[2,256,448]{1,2,0:T(8,128)}, f32[2,256,448]{1,2,0:T(8,128)S(1)}, u32[]{:S(2)}, u32[]{:S(2)}) collective-permute-start(f32[2,256,448]{1,2,0:T(8,128)} %copy.65), channel_id=1, source_target_pairs={{0,4},{4,0},{1,5},{5,1},{2,6},{6,2},{3,7},{7,3},{8,12},{12,8},{9,1... | collective-permute-start | bytes 2752520 | tf_op jit(solution)/shard_map/ppermute | solution.py:17
  232.4 20.3 %copy-start.2 = (bf16[2,256,896]{2,1,0:T(8,128)(2,1)S(1)}, bf16[2,256,896]{2,1,0:T(8,128)(2,1)}, u32[]{:S(2)}) copy-start(bf16[2,256,896]{2,1,0:T(8,128)(2,1)} %copy-done.1) | copy-start | bytes 2752516
  232.4 14.3 %collective-permute-start.16 = (f32[2,256,224]{2,1,0:T(8,128)}, f32[2,256,224]{2,1,0:T(8,128)S(1)}, u32[]{:S(2)}, u32[]{:S(2)}) collective-permute-start(f32[2,256,224]{2,1,0:T(8,128)} %slice_select_fusion), channel_id=1, source_target_pairs={{0,2},{2,0},{1,3},{3,1},{4,6},{6,4},{5,7},{7,5},{8,10},{10,8},{9,1... | collective-permute-start | bytes 1376264 | tf_op jit(solution)/shard_map/ppermute | solution.py:17
  246.9 12.0 %copy-start.9 = (bf16[2,256,256]{2,1,0:T(8,128)(2,1)S(1)}, bf16[2,256,256]{2,1,0:T(8,128)(2,1)}, u32[]{:S(2)}) copy-start(bf16[2,256,256]{2,1,0:T(8,128)(2,1)} %copy-done.8) | copy-start | bytes 786436
  247.1 7.7 %collective-permute-start.17 = (f32[2,256,112]{2,1,0:T(8,128)S(1)}, f32[2,256,112]{2,1,0:T(8,128)S(1)}, u32[]{:S(2)}, u32[]{:S(2)}) collective-permute-start(f32[2,256,112]{2,1,0:T(8,128)S(1)} %slice_select_fusion.1), channel_id=1, source_target_pairs={{0,1},{1,0},{2,3},{3,2},{4,5},{5,4},{6,7},{7,6},{8,9},{9,8},{10,11... | collective-permute-start | bytes 688136 | tf_op jit(solution)/shard_map/ppermute | solution.py:17
  255.6 12.8 %all-to-all-start.1 = ((bf16[2,8,32,112]{3,2,0,1:T(8,128)(2,1)}), bf16[2,8,32,112]{3,2,0,1:T(8,128)(2,1)S(1)}, u32[]{:S(2)}, u32[]{:S(2)}) async-start(bf16[2,8,32,112]{3,2,0,1:T(8,128)(2,1)} %copy.67), calls=%async_computation.1 | async-start | bytes 262144 | tf_op jit(solution)/shard_map/all_to_all | solution.py:172
  282.2 1.0 copy-start.4
  282.2 0.9 copy-start.10
  (1 other events, 0.7 us)
where the time goes:
time: 289 us; the launch traced here: 288 us
  waiting for transfers between devices  108 us (37%)
  local copies, waits for them, and re-layouts  74.3 us (26%)
  starting transfers between devices  68.2 us (24%)
  blocking collectives  18.6 us (6%)
  other arithmetic  11.3 us (4%)
  matrix products  6.11 us (2%)
    ppermute x18, waiting for transfers between devices, from_partner(): return lax.ppermute(block, axis, route)  101 us
    ppermute x18, starting transfers between devices, from_partner(): return lax.ppermute(block, axis, route)  64.8 us
    all_to_all x1, blocking collectives, on_device(): lax.all_to_all(outgoing, 'node', split_axis=1, concat_axis=1, tiled=True)  18.6 us
    scatter x1, local copies, waits for them, and re-layouts, route_slots(): jnp.zeros((groups * capacity,), jnp.bool_).at[flat_target]  17.6 us
    scatter x1, local copies, waits for them, and re-layouts, route_slots(): jnp.zeros((groups * capacity,), jnp.int32).at[flat_target]  15.5 us
    scatter x1, local copies, waits for them, and re-layouts, route_slots(): slot_weight = jnp.zeros((groups * capacity,), jnp.float32).at[flat_target...  15.5 us
    gather x2, local copies, waits for them, and re-layouts, on_device(): picked = flat_back[:, safe_target]  14 us
    all_to_all x1, waiting for transfers between devices, on_device(): lax.all_to_all(reduced.reshape(2, groups, capacity, width_local), 'node',...  7.16 us
  transfers between devices with their start and end apart: 19, of which 10 were waited for; matrix products, arithmetic and copies ran while one was open for 2% of the time, Pallas kernels for 0%

commit v1 on v0

v1 whole, which is shorter than its diff:
```python
import jax
import jax.numpy as jnp
from jax import lax
from jax.experimental import pallas as pl
from jax.experimental.pallas import tpu as pltpu
from jax.sharding import PartitionSpec as P

EXPERTS = 256
CAP = 32
NODES = 8
MESH = pl.DeviceIdType.MESH
BF16 = jnp.bfloat16
F32 = jnp.float32


def nn(left, right):
    return lax.dot_general(left, right, (((1,), (0,)), ((), ())), preferred_element_type=F32)


def nt(left, right):
    return lax.dot_general(left, right, (((1,), (1,)), ((), ())), preferred_element_type=F32)


def kernel(
    tok, og, ids, wts, wg_h, wu_h, wd_h,
    lo, ig, gg_h, ug_h, dg_h,
    wg, wu, wd, wgt, wut, wdt, sel, a_src, a_dst, pieces,
    c_own, c_src, c_dst, y_src, y_dst, rows, e_src, e_dst, r_own, r_src, r_dst, f_src, f_dst,
    gg, ug, dg,
    w_sem, o_sem, as_sem, ar_sem, bs_sem, br_sem, gs_sem, gr_sem, cs_sem, cr_sem, ys_sem, yr_sem,
    ds_sem, dr_sem, es_sem, er_sem, rs_sem, rr_sem, fs_sem, fr_sem,
):
    node = lax.axis_index("node")
    lane = lax.axis_index("local")
    x, half, spot, core = lane // 16, (lane // 8) % 2, (lane // 2) % 4, lane % 2
    unit = lane % 8

    def place(x_at, half_at, spot_at, core_at):
        return {"node": node, "local": ((x_at * 2 + half_at) * 4 + spot_at) * 2 + core_at}

    z_peer = [{"node": (node + d) % NODES, "local": lane} for d in range(1, 8)]
    x_peer = [place((x + d) % 4, half, spot, core) for d in range(1, 4)]
    y_peer = [place(x, half, (spot + d) % 4, core) for d in range(1, 4)]
    twin = place(x, half, spot, 1 - core)
    far = place(x, 1 - half, spot, core)

    barrier = pltpu.get_barrier_semaphore()
    for peer in z_peer + x_peer + y_peer + [twin, far]:
        pl.semaphore_signal(barrier, inc=1, device_id=peer, device_id_type=MESH)

    sends = []

    def send(src, dst, s_sem, r_sem, peer):
        copy = pltpu.make_async_remote_copy(
            src_ref=src, dst_ref=dst, send_sem=s_sem, recv_sem=r_sem, device_id=peer, device_id_type=MESH
        )
        copy.start()
        sends.append(copy)
        return copy

    loads = [
        pltpu.make_async_copy(src, dst, w_sem.at[i])
        for i, (src, dst) in enumerate([(wg_h, wg), (wu_h, wu), (wd_h, wd)])
    ]
    for load in loads:
        load.start()

    match = (ids[...] & (EXPERTS // NODES - 1)) == 0
    hit = jnp.sum(jnp.where(match, 1.0, 0.0), axis=0, keepdims=True)
    owner = jnp.sum(jnp.where(match, ids[...] // (EXPERTS // NODES), 0), axis=0, keepdims=True)
    share = jnp.sum(jnp.where(match, wts[...], 0.0), axis=0, keepdims=True)
    count = tok.shape[1]
    mine = (lax.broadcasted_iota(jnp.int32, (16, count), 0) == owner) & (hit > 0.0)
    mine = jnp.where(mine, 1.0, 0.0)
    before = lax.broadcasted_iota(jnp.int32, (count, count), 0) < lax.broadcasted_iota(jnp.int32, (count, count), 1)
    rank = nn(mine.astype(BF16), jnp.where(before, 1.0, 0.0).astype(BF16))
    rank = jnp.sum(mine * rank, axis=0, keepdims=True).astype(jnp.int32)
    target = jnp.where(hit > 0.0, owner * CAP + rank, -1)
    chosen = lax.broadcasted_iota(jnp.int32, (NODES * CAP, count), 0) == target
    sel[...] = jnp.where(chosen, 1.0, 0.0).astype(BF16)

    def dispatch(s, source):
        slots = nt(sel[...], source).astype(BF16)
        width = slots.shape[1]
        a_src[s, :, :, 0:width] = slots.reshape(NODES, CAP, width)
        a_dst[s, node] = a_src[s, node]
        return [
            send(a_src.at[s, (node + d) % NODES], a_dst.at[s, node], as_sem.at[s, d - 1], ar_sem.at[s, d - 1], z_peer[d - 1])
            for d in range(1, 8)
        ]

    width = tok.shape[0]

    def landed(s, copies):
        for copy in copies:
            copy.wait_recv()
        block = a_dst[s, :, :, 0:width].reshape(NODES * CAP, width)
        pieces[s, unit] = block.T
        own = pieces.at[s, unit]
        to_twin = send(own, own, gs_sem.at[s, 0], gr_sem.at[s, 0], twin)
        to_line = [send(own, own, bs_sem.at[s, d - 1], br_sem.at[s, d - 1], y_peer[d - 1]) for d in range(1, 4)]
        return to_twin, to_line

    def forward(s, to_line):
        shared = []
        for d in range(1, 4):
            to_line[d - 1].wait_recv()
            block = pieces.at[s, ((spot + 4 - d) % 4) * 2 + core]
            shared.append(send(block, block, gs_sem.at[s, d], gr_sem.at[s, d], twin))
        return shared

    def whole(s):
        return pieces[s].reshape(8 * width, NODES * CAP)

    hid_x = 64

    def scatter(s, first, parts):
        for i, part in enumerate(parts):
            split = part.reshape(4, hid_x, NODES * CAP)
            c_own[:, first + i] = split
            c_src[:, first + i] = split.astype(BF16)
        span = pl.ds(first, len(parts))
        return [
            send(c_src.at[(x + d) % 4, span], c_dst.at[d - 1, span], cs_sem.at[s, d - 1], cr_sem.at[s, d - 1], x_peer[d - 1])
            for d in range(1, 4)
        ]

    def across(s, first, number, copies):
        total = [c_own[x, first + i] for i in range(number)]
        for d in range(1, 4):
            copies[d - 1].wait_recv()
            total = [total[i] + c_dst[d - 1, first + i].astype(F32) for i in range(number)]
        for i in range(number):
            y_src[first + i] = total[i].astype(BF16)
        span = pl.ds(first, number)
        copy = send(y_src.at[span], y_dst.at[span], ys_sem.at[s], yr_sem.at[s], far)
        return total, copy

    def complete(first, total, copy):
        copy.wait_recv()
        return [part + y_dst[first + i].astype(F32) for i, part in enumerate(total)]

    def spread(s, first, values):
        for i, value in enumerate(values):
            rows[x, first + i] = value
        block = rows.at[x, pl.ds(first, len(values))]
        return [send(block, block, ds_sem.at[s, d - 1], dr_sem.at[s, d - 1], x_peer[d - 1]) for d in range(1, 4)]

    def gathered(i):
        return rows[:, i].reshape(4 * hid_x, NODES * CAP)

    def weight_half(weight, which):
        return weight[:, which].reshape(4 * width, weight.shape[3])

    def pair_sum(s, terms):
        def part(which):
            return sum(nn(weight_half(weight, which), value) for weight, value in terms)

        e_src[s] = part(1 - core).reshape(4, width, NODES * CAP).astype(BF16)
        copy = send(e_src.at[s], e_dst.at[s], es_sem.at[s], er_sem.at[s], twin)
        own = part(core).reshape(4, width, NODES * CAP)
        return own, copy

    def line_sum(s, own, copy):
        copy.wait_recv()
        total = own + e_dst[s].astype(F32)
        r_own[s] = total
        r_src[s] = total.astype(BF16)
        return [
            send(r_src.at[s, (spot + d) % 4], r_dst.at[s, d - 1], rs_sem.at[s, d - 1], rr_sem.at[s, d - 1], y_peer[d - 1])
            for d in range(1, 4)
        ]

    def give_back(s, copies):
        total = r_own[s, spot]
        for d in range(1, 4):
            copies[d - 1].wait_recv()
            total = total + r_dst[s, d - 1].astype(F32)
        f_src[s, :, :, 0:width] = total.astype(BF16).T.reshape(NODES, CAP, width)
        f_dst[s, node] = f_src[s, node]
        return [
            send(f_src.at[s, (node + d) % NODES], f_dst.at[s, node], fs_sem.at[s, d - 1], fr_sem.at[s, d - 1], z_peer[d - 1])
            for d in range(1, 8)
        ]

    def combine(s, copies):
        for copy in copies:
            copy.wait_recv()
        block = f_dst[s, :, :, 0:width].reshape(NODES * CAP, width)
        return nn(block.T, sel[...])

    pl.semaphore_wait(barrier, 15)
    a_tok = dispatch(0, tok[...])
    a_grad = dispatch(1, (share * og[...].astype(F32)).astype(BF16))

    for load in loads:
        load.wait()
    hidden_units = wd.shape[0]
    wgt[...] = wg[...].reshape(8 * width, hidden_units).T
    wut[...] = wu[...].reshape(8 * width, hidden_units).T
    wdt[...] = wd[...].T.reshape(4, 2, width, hidden_units)

    twin_tok, line_tok = landed(0, a_tok)
    shared_tok = forward(0, line_tok)
    twin_grad, line_grad = landed(1, a_grad)
    for copy in [twin_tok] + shared_tok:
        copy.wait_recv()
    tokens_t = whole(0)
    c_fwd = scatter(0, 0, [nn(wgt[...], tokens_t), nn(wut[...], tokens_t)])
    sum_fwd, far_fwd = across(0, 0, 2, c_fwd)
    shared_grad = forward(1, line_grad)
    for copy in [twin_grad] + shared_grad:
        copy.wait_recv()
    c_bwd = scatter(1, 2, [nn(wd[...], whole(1))])
    gate_sum, up_sum = complete(0, sum_fwd, far_fwd)
    sig = jax.nn.sigmoid(gate_sum)
    active = gate_sum * sig
    d_fwd = spread(0, 0, [(active * up_sum).astype(BF16)])
    sum_bwd, far_bwd = across(1, 2, 1, c_bwd)
    for copy in d_fwd:
        copy.wait_recv()
    own_fwd, e_fwd = pair_sum(0, [(wdt, gathered(0))])
    (back_sum,) = complete(2, sum_bwd, far_bwd)
    grad_gate = (back_sum * up_sum * sig * (1.0 + gate_sum * (1.0 - sig))).astype(BF16)
    grad_up = (back_sum * active).astype(BF16)
    d_bwd = spread(1, 1, [grad_gate, grad_up])
    r_fwd = line_sum(0, own_fwd, e_fwd)
    dg[...] = nt(gathered(0), whole(1)).astype(BF16)
    stores = [pltpu.make_async_copy(dg, dg_h, o_sem.at[0])]
    stores[0].start()
    for copy in d_bwd:
        copy.wait_recv()
    own_bwd, e_bwd = pair_sum(1, [(wg, gathered(1)), (wu, gathered(2))])
    r_bwd = line_sum(1, own_bwd, e_bwd)
    gg[...] = nt(whole(0), gathered(1)).astype(BF16)
    ug[...] = nt(whole(0), gathered(2)).astype(BF16)
    stores += [pltpu.make_async_copy(gg, gg_h, o_sem.at[1]), pltpu.make_async_copy(ug, ug_h, o_sem.at[2])]
    stores[1].start()
    stores[2].start()
    f_fwd = give_back(0, r_fwd)
    f_bwd = give_back(1, r_bwd)
    lo[...] = (share * combine(0, f_fwd)).astype(BF16)
    ig[...] = combine(1, f_bwd).astype(BF16)
    for copy in sends:
        copy.wait_send()
    for store in stores:
        store.wait()


def on_device(tokens, out_grad, route_ids, route_weights, gate_weight, up_weight, down_weight):
    count, width = tokens.shape
    units, hid = gate_weight.shape[2], gate_weight.shape[3]
    slots = NODES * CAP
    vmem = pl.BlockSpec(memory_space=pltpu.VMEM)
    hbm = pl.BlockSpec(memory_space=pl.ANY)
    dma = pltpu.SemaphoreType.DMA
    shapes = [
        ((4, 2, width, hid), BF16),
        ((4, 2, width, hid), BF16),
        ((hid, units), BF16),
        ((hid, units), BF16),
        ((hid, units), BF16),
        ((4, 2, width, hid), BF16),
        ((slots, count), BF16),
        ((2, NODES, CAP, 128), BF16),
        ((2, NODES, CAP, 128), BF16),
        ((2, 8, width, slots), BF16),
        ((4, 3, hid // 4, slots), F32),
        ((4, 3, hid // 4, slots), BF16),
        ((3, 3, hid // 4, slots), BF16),
        ((3, hid // 4, slots), BF16),
        ((3, hid // 4, slots), BF16),
        ((4, 3, hid // 4, slots), BF16),
        ((2, 4, width, slots), BF16),
        ((2, 4, width, slots), BF16),
        ((2, 4, width, slots), F32),
        ((2, 4, width, slots), BF16),
        ((2, 3, width, slots), BF16),
        ((2, NODES, CAP, 128), BF16),
        ((2, NODES, CAP, 128), BF16),
        ((units, hid), BF16),
        ((units, hid), BF16),
        ((hid, units), BF16),
    ]
    sems = [(3,), (3,), (2, 7), (2, 7), (2, 3), (2, 3), (2, 4), (2, 4), (2, 3), (2, 3), (2,), (2,)]
    sems += [(2, 3), (2, 3), (2,), (2,), (2, 3), (2, 3), (2, 7), (2, 7)]
    lo, ig, gg, ug, dg = pl.pallas_call(
        kernel,
        out_shape=(
            jax.ShapeDtypeStruct((width, count), BF16),
            jax.ShapeDtypeStruct((width, count), BF16),
            jax.ShapeDtypeStruct((units, hid), BF16),
            jax.ShapeDtypeStruct((units, hid), BF16),
            jax.ShapeDtypeStruct((hid, units), BF16),
        ),
        in_specs=[vmem] * 4 + [hbm] * 3,
        out_specs=(vmem, vmem, hbm, hbm, hbm),
        scratch_shapes=[pltpu.VMEM(shape, kind) for shape, kind in shapes] + [dma(shape) for shape in sems],
        compiler_params=pltpu.CompilerParams(collective_id=0, has_side_effects=True, vmem_limit_bytes=40 << 20),
        name="expert_layer",
    )(
        tokens.T,
        out_grad.T,
        route_ids.T,
        route_weights.T,
        gate_weight.reshape(4, 2, width, hid),
        up_weight.reshape(4, 2, width, hid),
        down_weight.reshape(hid, units),
    )
    return (lo.T, ig.T, gg[None, None], ug[None, None], dg[None, None])


def solution(mesh):
    rows = P("node", "local")
    routes = P("node", None)
    blocks = P("node", "local", None, None)
    return jax.shard_map(
        on_device,
        mesh=mesh,
        in_specs=(rows, rows, routes, routes, blocks, blocks, blocks),
        out_specs=(rows, rows, blocks, blocks, blocks),
        check_vma=False,
    )
```

time: 289 us -> 72.9 us (0.25)
  waiting for transfers between devices: 108 us -> 0 us
  starting transfers between devices: 68.2 us -> 0 us
  local copies, waits for them, and re-layouts: 74.3 us -> 9.87 us
  Pallas kernels: 0 us -> 61.3 us
  blocking collectives: 18.6 us -> 0 us
  other arithmetic: 11.3 us -> 0 us
  matrix products: 6.11 us -> 0 us
    ppermute x18 -> x0, waiting for transfers between devices: 101 us -> none  [from_partner(): return lax.ppermute(block, axis, route)]
    ppermute x18 -> x0, starting transfers between devices: 64.8 us -> none  [from_partner(): return lax.ppermute(block, axis, route)]
    pallas_call x0 -> x1, Pallas kernels: none -> 61.3 us  [on_device(): pl.pallas_call(kernel, out_shape=(jax.ShapeDtypeStruct((width, count), BF...]
    scatter x3 -> x0, local copies, waits for them, and re-layouts: 48.6 us -> none  [the longest x1 17.6 us: route_slots(): jnp.zeros((groups * capacity,), jnp.bool_).at[flat_target]]
    all_to_all x1 -> x0, blocking collectives: 18.6 us -> none  [on_device(): lax.all_to_all(outgoing, 'node', split_axis=1, concat_axis=1, tiled=True)]
    gather x4 -> x0, local copies, waits for them, and re-layouts: 15.7 us -> none  [the longest x2 14 us: on_device(): picked = flat_back[:, safe_target]]
    all_to_all x1 -> x0, waiting for transfers between devices: 7.16 us -> none  [on_device(): lax.all_to_all(reduced.reshape(2, groups, capacity, width_local), 'node',...]
    dot_general x9 -> x0, matrix products: 6.11 us -> none  [the longest x6 5.21 us: contract(): lax.dot_general(left_side, right_side, (((left_dim,), (right_dim,)), ((),...]
  transfers between devices with their start and end apart: 19 -> 0, of which waited for: 10 -> 0; matrix products, arithmetic and copies ran while one was open for 2% -> 0% of each run, Pallas kernels for 0% -> 0%
where the time goes in v1:
time: 72.9 us; the launch traced here: 71.9 us
  Pallas kernels  61.3 us (84%)
  local copies, waits for them, and re-layouts  9.87 us (14%)
    pallas_call x1, Pallas kernels, on_device(): pl.pallas_call(kernel, out_shape=(jax.ShapeDtypeStruct((width, count), BF...  61.3 us
    unnamed x19, local copies, waits for them, and re-layouts  9.87 us

profile of v1, /device:TPU:1, one launch (start us, length us, event | category | flops | bytes accessed | tf_op | source)
XLA Modules:
  0.0 71.9 jit_solution(3803503787602765863)
XLA Ops:
  0.6 0.0 copy-start
  0.6 1.0 %copy-done = bf16[1,1,896,256]{3,2,1,0:T(8,128)(2,1)S(1)} copy-done((bf16[1,1,896,256]{3,2,1,0:T(8,128)(2,1)S(1)}, bf16[1,1,896,256]{3,2,1,0:T(8,128)(2,1)}, u32[]{:S(2)}) %copy-start) | copy-done | bytes 458776
  1.7 0.0 copy-start.1
  1.7 1.0 %copy-done.1 = bf16[1,1,896,256]{3,2,1,0:T(8,128)(2,1)S(1)} copy-done((bf16[1,1,896,256]{3,2,1,0:T(8,128)(2,1)S(1)}, bf16[1,1,896,256]{3,2,1,0:T(8,128)(2,1)}, u32[]{:S(2)}) %copy-start.1) | copy-done | bytes 458776
  2.7 0.0 copy-start.2
  2.7 1.0 %copy-done.2 = bf16[1,1,256,896]{3,2,1,0:T(8,128)(2,1)S(1)} copy-done((bf16[1,1,256,896]{3,2,1,0:T(8,128)(2,1)S(1)}, bf16[1,1,256,896]{3,2,1,0:T(8,128)(2,1)}, u32[]{:S(2)}) %copy-start.2) | copy-done | bytes 458776
  3.7 0.0 copy-start.3
  3.7 0.9 %copy-done.3 = bf16[512,112]{0,1:T(8,128)(2,1)S(1)} copy-done((bf16[512,112]{0,1:T(8,128)(2,1)S(1)}, bf16[512,112]{0,1:T(8,128)(2,1)}, u32[]{:S(2)}) %copy-start.3) | copy-done | bytes 114712
  4.6 0.0 copy-start.4
  4.6 0.9 %copy-done.4 = bf16[512,112]{0,1:T(8,128)(2,1)S(1)} copy-done((bf16[512,112]{0,1:T(8,128)(2,1)S(1)}, bf16[512,112]{0,1:T(8,128)(2,1)}, u32[]{:S(2)}) %copy-start.4) | copy-done | bytes 114712
  5.5 0.0 copy-start.5
  5.5 0.7 copy-done.5
  6.2 0.0 copy-start.6
  6.2 0.7 copy-done.6
  6.9 61.3 %expert_layer.1 = (bf16[112,512]{1,0:T(8,128)(2,1)S(1)}, bf16[112,512]{1,0:T(8,128)(2,1)S(1)}, bf16[896,256]{1,0:T(8,128)(2,1)S(1)}, bf16[896,256]{1,0:T(8,128)(2,1)S(1)}, bf16[256,896]{1,0:T(8,128)(2,1)S(1)}) custom-call(bf16[112,512]{1,0:T(8,128)(2,1)S(1)} %bitcast.18, bf16[112,512]{1,0:T(8,128)(2,1)S(1)} %bitcast.19, s32[8,512]{1,0:T(8,128)S(1)} %bitcast.22, ...), custom_call_target="tpu_custom_call" | custom-call | tf_op jit(solution)/shard_map/expert_layer/pallas_call | solution.py:287
  68.3 0.6 copy.17
  68.9 0.6 copy.18
  69.6 0.8 %copy.19 = bf16[1,1,896,256]{3,2,1,0:T(8,128)(2,1)} copy(bf16[1,1,896,256]{3,2,1,0:T(8,128)(2,1)S(1)} %bitcast.14) | data formatting | bytes 917504
  70.3 0.8 %copy.20 = bf16[1,1,896,256]{3,2,1,0:T(8,128)(2,1)} copy(bf16[1,1,896,256]{3,2,1,0:T(8,128)(2,1)S(1)} %bitcast.13) | data formatting | bytes 917504
  71.1 0.8 %copy.21 = bf16[1,1,256,896]{3,2,1,0:T(8,128)(2,1)} copy(bf16[1,1,256,896]{3,2,1,0:T(8,128)(2,1)S(1)} %bitcast.12) | data formatting | bytes 917504
Async XLA Ops:
  0.6 1.0 %copy-start = (bf16[1,1,896,256]{3,2,1,0:T(8,128)(2,1)S(1)}, bf16[1,1,896,256]{3,2,1,0:T(8,128)(2,1)}, u32[]{:S(2)}) copy-start(bf16[1,1,896,256]{3,2,1,0:T(8,128)(2,1)} %param.11) | copy-start | bytes 1376260
  1.7 1.0 %copy-start.1 = (bf16[1,1,896,256]{3,2,1,0:T(8,128)(2,1)S(1)}, bf16[1,1,896,256]{3,2,1,0:T(8,128)(2,1)}, u32[]{:S(2)}) copy-start(bf16[1,1,896,256]{3,2,1,0:T(8,128)(2,1)} %param.12) | copy-start | bytes 1376260
  2.7 1.0 %copy-start.2 = (bf16[1,1,256,896]{3,2,1,0:T(8,128)(2,1)S(1)}, bf16[1,1,256,896]{3,2,1,0:T(8,128)(2,1)}, u32[]{:S(2)}) copy-start(bf16[1,1,256,896]{3,2,1,0:T(8,128)(2,1)} %param.13) | copy-start | bytes 1376260
  3.7 0.9 %copy-start.3 = (bf16[512,112]{0,1:T(8,128)(2,1)S(1)}, bf16[512,112]{0,1:T(8,128)(2,1)}, u32[]{:S(2)}) copy-start(bf16[512,112]{0,1:T(8,128)(2,1)} %param.7) | copy-start | bytes 344068
  4.6 0.9 %copy-start.4 = (bf16[512,112]{0,1:T(8,128)(2,1)S(1)}, bf16[512,112]{0,1:T(8,128)(2,1)}, u32[]{:S(2)}) copy-start(bf16[512,112]{0,1:T(8,128)(2,1)} %param.8) | copy-start | bytes 344068
  5.5 0.7 copy-start.5
  6.2 0.7 copy-start.6

commit v2 on v1

--- a/solution.py
+++ b/solution.py
@@ -7,6 +7,7 @@
 
 EXPERTS = 256
 CAP = 32
+VMEM_BYTES = 24 << 20
 NODES = 8
 MESH = pl.DeviceIdType.MESH
 BF16 = jnp.bfloat16
@@ -21,13 +22,17 @@
     return lax.dot_general(left, right, (((1,), (1,)), ((), ())), preferred_element_type=F32)
 
 
+def slot_numbers(count):
+    return lax.broadcasted_iota(jnp.int32, (NODES * CAP, count), 0).astype(F32)
+
+
 def kernel(
-    tok, og, ids, wts, wg_h, wu_h, wd_h,
-    lo, ig, gg_h, ug_h, dg_h,
+    tok_h, og_h, ids_h, wts_h, wg_h, wu_h, wd_h,
+    back, meta, gg, ug, dg,
+    tok, og, ids, wts,
     wg, wu, wd, wgt, wut, wdt, sel, a_src, a_dst, pieces,
     c_own, c_src, c_dst, y_src, y_dst, rows, e_src, e_dst, r_own, r_src, r_dst, f_src, f_dst,
-    gg, ug, dg,
-    w_sem, o_sem, as_sem, ar_sem, bs_sem, br_sem, gs_sem, gr_sem, cs_sem, cr_sem, ys_sem, yr_sem,
+    w_sem, as_sem, ar_sem, bs_sem, br_sem, gs_sem, gr_sem, cs_sem, cr_sem, ys_sem, yr_sem,
     ds_sem, dr_sem, es_sem, er_sem, rs_sem, rr_sem, fs_sem, fr_sem,
 ):
     node = lax.axis_index("node")
@@ -60,10 +65,14 @@
 
     loads = [
         pltpu.make_async_copy(src, dst, w_sem.at[i])
-        for i, (src, dst) in enumerate([(wg_h, wg), (wu_h, wu), (wd_h, wd)])
+        for i, (src, dst) in enumerate(
+            [(ids_h, ids), (wts_h, wts), (tok_h, tok), (og_h, og), (wg_h, wg), (wu_h, wu), (wd_h, wd)]
+        )
     ]
     for load in loads:
         load.start()
+    loads[0].wait()
+    loads[1].wait()
 
     match = (ids[...] & (EXPERTS // NODES - 1)) == 0
     hit = jnp.sum(jnp.where(match, 1.0, 0.0), axis=0, keepdims=True)
@@ -75,9 +84,11 @@
     before = lax.broadcasted_iota(jnp.int32, (count, count), 0) < lax.broadcasted_iota(jnp.int32, (count, count), 1)
     rank = nn(mine.astype(BF16), jnp.where(before, 1.0, 0.0).astype(BF16))
     rank = jnp.sum(mine * rank, axis=0, keepdims=True).astype(jnp.int32)
-    target = jnp.where(hit > 0.0, owner * CAP + rank, -1)
-    chosen = lax.broadcasted_iota(jnp.int32, (NODES * CAP, count), 0) == target
+    target = jnp.where(hit > 0.0, (owner * CAP + rank).astype(F32), -1.0)
+    chosen = slot_numbers(count) == target
     sel[...] = jnp.where(chosen, 1.0, 0.0).astype(BF16)
+    meta[0:1] = target
+    meta[1:2] = share
 
     def dispatch(s, source):
         slots = nt(sel[...], source).astype(BF16)
@@ -183,17 +194,13 @@
             for d in range(1, 8)
         ]
 
-    def combine(s, copies):
-        for copy in copies:
-            copy.wait_recv()
-        block = f_dst[s, :, :, 0:width].reshape(NODES * CAP, width)
-        return nn(block.T, sel[...])
-
     pl.semaphore_wait(barrier, 15)
+    loads[2].wait()
     a_tok = dispatch(0, tok[...])
+    loads[3].wait()
     a_grad = dispatch(1, (share * og[...].astype(F32)).astype(BF16))
 
-    for load in loads:
+    for load in loads[4:]:
         load.wait()
     hidden_units = wd.shape[0]
     wgt[...] = wg[...].reshape(8 * width, hidden_units).T
@@ -226,25 +233,33 @@
     d_bwd = spread(1, 1, [grad_gate, grad_up])
     r_fwd = line_sum(0, own_fwd, e_fwd)
     dg[...] = nt(gathered(0), whole(1)).astype(BF16)
-    stores = [pltpu.make_async_copy(dg, dg_h, o_sem.at[0])]
-    stores[0].start()
     for copy in d_bwd:
         copy.wait_recv()
     own_bwd, e_bwd = pair_sum(1, [(wg, gathered(1)), (wu, gathered(2))])
     r_bwd = line_sum(1, own_bwd, e_bwd)
     gg[...] = nt(whole(0), gathered(1)).astype(BF16)
     ug[...] = nt(whole(0), gathered(2)).astype(BF16)
-    stores += [pltpu.make_async_copy(gg, gg_h, o_sem.at[1]), pltpu.make_async_copy(ug, ug_h, o_sem.at[2])]
-    stores[1].start()
-    stores[2].start()
     f_fwd = give_back(0, r_fwd)
     f_bwd = give_back(1, r_bwd)
-    lo[...] = (share * combine(0, f_fwd)).astype(BF16)
-    ig[...] = combine(1, f_bwd).astype(BF16)
+    for copy in f_fwd + f_bwd:
+        copy.wait_recv()
+    back[...] = f_dst[...]
     for copy in sends:
         copy.wait_send()
-    for store in stores:
-        store.wait()
+
+
+def finish(back, meta, gg, ug, dg, lo, ig, gg_h, ug_h, dg_h, sems):
+    copies = [
+        pltpu.make_async_copy(src, dst, sems.at[i]) for i, (src, dst) in enumerate([(gg, gg_h), (ug, ug_h), (dg, dg_h)])
+    ]
+    for copy in copies:
+        copy.start()
+    width, count = lo.shape
+    sel = jnp.where(slot_numbers(count) == meta[0:1], 1.0, 0.0).astype(BF16)
+    lo[...] = (meta[1:2] * nn(back[0, :, :, 0:width].reshape(NODES * CAP, width).T, sel)).astype(BF16)
+    ig[...] = nn(back[1, :, :, 0:width].reshape(NODES * CAP, width).T, sel).astype(BF16)
+    for copy in copies:
+        copy.wait()
 
 
 def on_device(tokens, out_grad, route_ids, route_weights, gate_weight, up_weight, down_weight):
@@ -252,9 +267,13 @@
     units, hid = gate_weight.shape[2], gate_weight.shape[3]
     slots = NODES * CAP
     vmem = pl.BlockSpec(memory_space=pltpu.VMEM)
-    hbm = pl.BlockSpec(memory_space=pl.ANY)
+    hbm = pl.BlockSpec(memory_space=pltpu.HBM)
     dma = pltpu.SemaphoreType.DMA
     shapes = [
+        ((width, count), BF16),
+        ((width, count), BF16),
+        (route_ids.shape[::-1], jnp.int32),
+        (route_ids.shape[::-1], F32),
         ((4, 2, width, hid), BF16),
         ((4, 2, width, hid), BF16),
         ((hid, units), BF16),
@@ -278,27 +297,10 @@
         ((2, 3, width, slots), BF16),
         ((2, NODES, CAP, 128), BF16),
         ((2, NODES, CAP, 128), BF16),
-        ((units, hid), BF16),
-        ((units, hid), BF16),
-        ((hid, units), BF16),
     ]
-    sems = [(3,), (3,), (2, 7), (2, 7), (2, 3), (2, 3), (2, 4), (2, 4), (2, 3), (2, 3), (2,), (2,)]
+    sems = [(7,), (2, 7), (2, 7), (2, 3), (2, 3), (2, 4), (2, 4), (2, 3), (2, 3), (2,), (2,)]
     sems += [(2, 3), (2, 3), (2,), (2,), (2, 3), (2, 3), (2, 7), (2, 7)]
-    lo, ig, gg, ug, dg = pl.pallas_call(
-        kernel,
-        out_shape=(
-            jax.ShapeDtypeStruct((width, count), BF16),
-            jax.ShapeDtypeStruct((width, count), BF16),
-            jax.ShapeDtypeStruct((units, hid), BF16),
-            jax.ShapeDtypeStruct((units, hid), BF16),
-            jax.ShapeDtypeStruct((hid, units), BF16),
-        ),
-        in_specs=[vmem] * 4 + [hbm] * 3,
-        out_specs=(vmem, vmem, hbm, hbm, hbm),
-        scratch_shapes=[pltpu.VMEM(shape, kind) for shape, kind in shapes] + [dma(shape) for shape in sems],
-        compiler_params=pltpu.CompilerParams(collective_id=0, has_side_effects=True, vmem_limit_bytes=40 << 20),
-        name="expert_layer",
-    )(
+    operands = (
         tokens.T,
         out_grad.T,
         route_ids.T,
@@ -307,6 +309,38 @@
         up_weight.reshape(4, 2, width, hid),
         down_weight.reshape(hid, units),
     )
+    back, meta, gg, ug, dg = pl.pallas_call(
+        kernel,
+        out_shape=(
+            jax.ShapeDtypeStruct((2, NODES, CAP, 128), BF16),
+            jax.ShapeDtypeStruct((8, count), F32),
+            jax.ShapeDtypeStruct((units, hid), BF16),
+            jax.ShapeDtypeStruct((units, hid), BF16),
+            jax.ShapeDtypeStruct((hid, units), BF16),
+        ),
+        in_specs=[hbm] * 7,
+        out_specs=(vmem,) * 5,
+        scratch_shapes=[pltpu.VMEM(shape, kind) for shape, kind in shapes] + [dma(shape) for shape in sems],
+        compiler_params=pltpu.CompilerParams(collective_id=0, has_side_effects=True, vmem_limit_bytes=VMEM_BYTES),
+        name="expert_layer",
+    )(
+        *(pltpu.with_memory_space_constraint(array, pltpu.HBM) for array in operands)
+    )
+    lo, ig, gg, ug, dg = pl.pallas_call(
+        finish,
+        out_shape=(
+            jax.ShapeDtypeStruct((width, count), BF16),
+            jax.ShapeDtypeStruct((width, count), BF16),
+            jax.ShapeDtypeStruct((units, hid), BF16),
+            jax.ShapeDtypeStruct((units, hid), BF16),
+            jax.ShapeDtypeStruct((hid, units), BF16),
+        ),
+        in_specs=[vmem] * 5,
+        out_specs=(vmem, vmem, hbm, hbm, hbm),
+        scratch_shapes=[dma((3,))],
+        compiler_params=pltpu.CompilerParams(vmem_limit_bytes=VMEM_BYTES),
+        name="finish",
+    )(back, meta, gg, ug, dg)
     return (lo.T, ig.T, gg[None, None], ug[None, None], dg[None, None])
 
 

time: 72.9 us -> 64.4 us (0.88)
  local copies, waits for them, and re-layouts: 9.87 us -> 0 us
  Pallas kernels: 61.3 us -> 63.3 us
    unnamed x19 -> x0, local copies, waits for them, and re-layouts: 9.87 us -> none
    pallas_call x1 -> x2, Pallas kernels: 61.3 us -> 63.3 us  [the longest x1 61.5 us: on_device(): pl.pallas_call(kernel, out_shape=(jax.ShapeDtypeStruct((2, NODES, CAP, 12...]
where the time goes in v2:
time: 64.4 us; the launch traced here: 63.9 us
  Pallas kernels  63.3 us (98%)
    pallas_call x1, Pallas kernels, on_device(): pl.pallas_call(kernel, out_shape=(jax.ShapeDtypeStruct((2, NODES, CAP, 12...  61.5 us
    pallas_call x1, Pallas kernels, on_device(): pl.pallas_call(finish, out_shape=(jax.ShapeDtypeStruct((width, count), BF...  1.82 us

profile of v2, /device:TPU:1, one launch (start us, length us, event | category | flops | bytes accessed | tf_op | source)
XLA Modules:
  0.0 63.9 jit_solution(5703346493558200516)
XLA Ops:
  0.6 61.5 %expert_layer.1 = (bf16[2,8,32,128]{3,2,1,0:T(8,128)(2,1)S(1)}, f32[8,512]{1,0:T(8,128)S(1)}, bf16[896,256]{1,0:T(8,128)(2,1)S(1)}, bf16[896,256]{1,0:T(8,128)(2,1)S(1)}, bf16[256,896]{1,0:T(8,128)(2,1)S(1)}) custom-call(bf16[112,512]{1,0:T(8,128)(2,1)} %bitcast.15, bf16[112,512]{1,0:T(8,128)(2,1)} %bitcast.16, s32[8,512]{1,0:T(8,128)} %bitcast.17, ...), custom_call_target="tpu_custom_call" | custom-call | tf_op jit(solution)/shard_map/expert_layer/pallas_call | solution.py:312
  62.1 1.8 %finish.1 = (bf16[112,512]{1,0:T(8,128)(2,1)}, bf16[112,512]{1,0:T(8,128)(2,1)}, bf16[896,256]{1,0:T(8,128)(2,1)}, bf16[896,256]{1,0:T(8,128)(2,1)}, bf16[256,896]{1,0:T(8,128)(2,1)}) custom-call(bf16[2,8,32,128]{3,2,1,0:T(8,128)(2,1)S(1)} %get-tuple-element.15.back, f32[8,512]{1,0:T(8,128)S(1)} %get-tuple-element.16.meta, ...), custom_call_target="tpu_custom_call" | custom-call | tf_op jit(solution)/shard_map/finish/pallas_call | solution.py:329

commit v3 on v2

v3 whole, which is shorter than its diff:
```python
import jax
import jax.numpy as jnp
from jax import lax
from jax.experimental import pallas as pl
from jax.experimental.pallas import tpu as pltpu
from jax.sharding import PartitionSpec as P

EXPERTS = 256
CAP = 32
VMEM_BYTES = 24 << 20
NODES = 8
MESH = pl.DeviceIdType.MESH
BF16 = jnp.bfloat16
F32 = jnp.float32


def nn(left, right):
    return lax.dot_general(left, right, (((1,), (0,)), ((), ())), preferred_element_type=F32)


def nt(left, right):
    return lax.dot_general(left, right, (((1,), (1,)), ((), ())), preferred_element_type=F32)


def slot_numbers(count):
    return lax.broadcasted_iota(jnp.int32, (NODES * CAP, count), 0).astype(F32)


STEPS = (0, 1, 7, 2, 6, 3, 5, 4)
RUNS = ((0, 4), (4, 8))


def kernel(
    tok_h, og_h, ids_h, wts_h, wg_h, wu_h, wd_h,
    back, meta, gg, ug, dg,
    tok, og, ids, wts, wg, wu, wd, wgt, wut, wdt, far_w, sel, a_src, a_dst, held,
    c_own, c_src, c_dst, y_own, y_src, y_dst, act, rows, r_own, r_src, r_dst, f_src, f_dst,
    w_sem, as_sem, ar_sem, bs_sem, br_sem, gs_sem, gr_sem, cs_sem, cr_sem, ys_sem, yr_sem,
    ds_sem, dr_sem, es_sem, er_sem, rs_sem, rr_sem, fs_sem, fr_sem, xs_sem, xr_sem,
):
    node = lax.axis_index("node")
    lane = lax.axis_index("local")
    x, half, spot, core = lane // 16, (lane // 8) % 2, (lane // 2) % 4, lane % 2
    unit = lane % 8

    def place(x_at, half_at, spot_at, core_at):
        return {"node": node, "local": ((x_at * 2 + half_at) * 4 + spot_at) * 2 + core_at}

    def after(j):
        return (node + STEPS[j]) % NODES

    def ahead(j):
        return (node + NODES - STEPS[j]) % NODES

    z_peer = [{"node": (node + d) % NODES, "local": lane} for d in range(1, 8)]
    x_peer = [place((x + d) % 4, half, spot, core) for d in range(1, 4)]
    y_peer = [place(x, half, (spot + d) % 4, core) for d in range(1, 4)]
    twin = place(x, half, spot, 1 - core)
    far = place(x, 1 - half, spot, core)

    barrier = pltpu.get_barrier_semaphore()
    for peer in z_peer + x_peer + y_peer + [twin, far]:
        pl.semaphore_signal(barrier, inc=1, device_id=peer, device_id_type=MESH)

    sends = []

    def send(src, dst, s_sem, r_sem, peer):
        copy = pltpu.make_async_remote_copy(
            src_ref=src, dst_ref=dst, send_sem=s_sem, recv_sem=r_sem, device_id=peer, device_id_type=MESH
        )
        copy.start()
        sends.append(copy)
        return copy

    width = tok_h.shape[0]
    units, hid = 8 * width, wd.shape[0]
    slots = NODES * CAP
    run = slots // 2
    count = tok.shape[1]
    loads = [
        pltpu.make_async_copy(src, dst, w_sem.at[i])
        for i, (src, dst) in enumerate(
            [
                (ids_h, ids),
                (wts_h, wts),
                (tok_h, tok.at[pl.ds(0, width)]),
                (og_h, og.at[pl.ds(0, width)]),
                (wg_h.at[:, 0], wg.at[0]),
                (wg_h.at[:, 1], wg.at[1]),
                (wu_h.at[:, 0], wu.at[0]),
                (wu_h.at[:, 1], wu.at[1]),
                (wd_h, wd),
            ]
        )
    ]
    for load in loads:
        load.start()
    tok[pl.ds(width, 128 - width)] = jnp.zeros((128 - width, count), BF16)
    og[pl.ds(width, 128 - width)] = jnp.zeros((128 - width, count), BF16)
    before = lax.broadcasted_iota(jnp.int32, (count, count), 0) < lax.broadcasted_iota(jnp.int32, (count, count), 1)
    before = jnp.where(before, 1.0, 0.0).astype(BF16)
    loads[0].wait()

    match = (ids[...] & (EXPERTS // NODES - 1)) == 0
    hit = jnp.sum(jnp.where(match, 1.0, 0.0), axis=0, keepdims=True)
    owner = jnp.sum(jnp.where(match, ids[...] // (EXPERTS // NODES), 0), axis=0, keepdims=True)
    mine = (lax.broadcasted_iota(jnp.int32, (16, count), 0) == owner) & (hit > 0.0)
    mine = jnp.where(mine, 1.0, 0.0)
    rank = nn(mine.astype(BF16), before)
    rank = jnp.sum(mine * rank, axis=0, keepdims=True)
    target = jnp.where(hit > 0.0, (owner * CAP).astype(F32) + rank, -1.0)
    sel[...] = jnp.where(slot_numbers(count) == target, 1.0, 0.0).astype(BF16)

    def dispatch(s, source):
        a_src[s] = nt(sel[...], source).astype(BF16).reshape(NODES, CAP, 128)
        copies = [None]
        for j in range(1, 8):
            peer = {"node": ahead(j), "local": lane}
            copies.append(send(a_src.at[s, ahead(j)], a_dst.at[s, j], as_sem.at[s, j - 1], ar_sem.at[s, j - 1], peer))
        a_dst[s, 0] = a_src[s, node]
        return copies

    def gather(s, h, copies):
        low, high = RUNS[h]
        for copy in copies[max(low, 1) : high]:
            copy.wait_recv()
        held[s, h, core, spot] = a_dst[s, low:high].reshape(run, 128).T[0:width]
        own = held.at[s, h, core, spot]
        to_line = [send(own, own, bs_sem.at[s, h, d - 1], br_sem.at[s, h, d - 1], y_peer[d - 1]) for d in range(1, 4)]
        to_twin = send(own, own, gs_sem.at[s, h, 0], gr_sem.at[s, h, 0], twin)
        return to_twin, to_line

    def forward(s, h, state):
        to_twin, to_line = state
        shared = [to_twin]
        for d in range(1, 4):
            to_line[d - 1].wait_recv()
            block = held.at[s, h, core, (spot + 4 - d) % 4]
            shared.append(send(block, block, gs_sem.at[s, h, d], gr_sem.at[s, h, d], twin))
        return shared

    def in_order(blocks):
        return jnp.concatenate([blocks(k, p) for p in range(4) for k in range(2)], axis=0)

    def whole(s, h):
        return in_order(lambda k, p: held[s, h, k, p])

    def all_rows(part):
        return jnp.concatenate([part(h) for h in range(2)], axis=1)

    def scatter(s, h, first, parts):
        for i, part in enumerate(parts):
            split = part.reshape(4, hid // 4, run)
            c_own[h, :, first + i] = split
            c_src[h, :, first + i] = split.astype(BF16)
        span = pl.ds(first, len(parts))
        return [
            send(
                c_src.at[h, (x + d) % 4, span],
                c_dst.at[h, d - 1, span],
                cs_sem.at[s, h, d - 1],
                cr_sem.at[s, h, d - 1],
                x_peer[d - 1],
            )
            for d in range(1, 4)
        ]

    def across(s, h, first, number, copies):
        span = slice(first, first + number)
        total = c_own[h, x, span]
        for d in range(1, 4):
            copies[d - 1].wait_recv()
            total = total + c_dst[h, d - 1, span].astype(F32)
        y_src[h, span] = total.astype(BF16)
        y_own[h, span] = total
        span = pl.ds(first, number)
        return send(y_src.at[h, span], y_dst.at[h, span], ys_sem.at[s, h], yr_sem.at[s, h], far)

    def complete(h, first, number, copy):
        copy.wait_recv()
        return [y_own[h, first + i] + y_dst[h, first + i].astype(F32) for i in range(number)]

    def spread(s, h, first, values):
        for i, value in enumerate(values):
            rows[h, core, x, first + i] = value
        span = pl.ds(first, len(values))
        block = rows.at[h, core, x, span]
        out = [send(block, block, ds_sem.at[s, h, d - 1], dr_sem.at[s, h, d - 1], x_peer[d - 1]) for d in range(1, 4)]
        shared = [send(block, block, es_sem.at[s, h, 0], er_sem.at[s, h, 0], twin)]
        return span, out, shared

    def pass_on(s, h, state):
        span, out, shared = state
        for d in range(1, 4):
            out[d - 1].wait_recv()
            block = rows.at[h, core, (x + 4 - d) % 4, span]
            shared.append(send(block, block, es_sem.at[s, h, d], er_sem.at[s, h, d], twin))
        return shared

    def gathered(h, which, i):
        return rows[h, which, :, i].reshape(hid, run)

    def line_sum(s, h, terms, shared):
        total = sum(nn(own[core].reshape(4 * width, hid), gathered(h, core, i)) for i, own, _ in terms)
        for copy in shared:
            copy.wait_recv()
        total += sum(nn(far_w[f].reshape(4 * width, hid), gathered(h, 1 - core, i)) for i, _, f in terms)
        total = total.reshape(4, width, run)
        r_src[s, h] = total.astype(BF16)
        r_own[s, h] = total
        return [
            send(
                r_src.at[s, h, (spot + d) % 4],
                r_dst.at[s, h, d - 1],
                rs_sem.at[s, h, d - 1],
                rr_sem.at[s, h, d - 1],
                y_peer[d - 1],
            )
            for d in range(1, 4)
        ]

    def give_back(s, h, copies):
        low, high = RUNS[h]
        total = r_own[s, h, spot]
        for d in range(1, 4):
            copies[d - 1].wait_recv()
            total = total + r_dst[s, h, d - 1].astype(F32)
        f_src[s, low:high, :, 0:width] = total.astype(BF16).T.reshape(high - low, CAP, width)
        out = []
        for j in range(max(low, 1), high):
            peer = {"node": after(j), "local": lane}
            out.append(send(f_src.at[s, j], f_dst.at[s, node], fs_sem.at[s, j - 1], fr_sem.at[s, j - 1], peer))
        if low == 0:
            f_dst[s, node] = f_src[s, 0]
        return out

    pl.semaphore_wait(barrier, 15)
    loads[2].wait()
    a_tok = dispatch(0, tok[...])
    loads[1].wait()
    share = jnp.sum(jnp.where(match, wts[...], 0.0), axis=0, keepdims=True)
    loads[3].wait()
    a_grad = dispatch(1, (share * og[...].astype(F32)).astype(BF16))
    meta[0:1] = target
    meta[1:2] = share

    for load in loads[4:]:
        load.wait()
    wdt_full = wd[...].T.reshape(4, 2, width, hid)
    wdt[0] = wdt_full[:, 0]
    wdt[1] = wdt_full[:, 1]
    far_copies = [
        send(weight.at[1 - core], far_w.at[i], xs_sem.at[i], xr_sem.at[i], twin) for i, weight in enumerate((wdt, wg, wu))
    ]
    wgt[...] = in_order(lambda k, p: wg[k, p]).T
    wut[...] = in_order(lambda k, p: wu[k, p]).T
    b_tok = [gather(0, h, a_tok) for h in range(2)]
    b_tok = [forward(0, h, b_tok[h]) for h in range(2)]
    b_grad = [gather(1, h, a_grad) for h in range(2)]
    c_fwd, c_bwd, y_fwd, y_bwd, d_fwd, d_bwd = [], [], [], [], [], []
    for h in range(2):
        for copy in b_tok[h]:
            copy.wait_recv()
        tokens = whole(0, h)
        c_fwd.append(scatter(0, h, 0, [nn(wgt[...], tokens), nn(wut[...], tokens)]))

    def activate(h):
        gate_sum, up_sum = complete(h, 0, 2, y_fwd[h])
        sig = jax.nn.sigmoid(gate_sum)
        active = gate_sum * sig
        d_fwd.append(spread(0, h, 0, [(active * up_sum).astype(BF16)]))
        act[h, 0] = up_sum * sig * (1.0 + gate_sum * (1.0 - sig))
        act[h, 1] = active

    def differentiate(h):
        (back_sum,) = complete(h, 2, 1, y_bwd[h])
        d_bwd.append(spread(1, h, 1, [(back_sum * act[h, 0]).astype(BF16), (back_sum * act[h, 1]).astype(BF16)]))

    for h in range(2):
        b_grad[h] = forward(1, h, b_grad[h])
        y_fwd.append(across(0, h, 0, 2, c_fwd[h]))
        for copy in b_grad[h]:
            copy.wait_recv()
        c_bwd.append(scatter(1, h, 2, [nn(wd[...], whole(1, h))]))
    for h in range(2):
        y_bwd.append(across(1, h, 2, 1, c_bwd[h]))
        activate(h)
    for copy in far_copies:
        copy.wait_recv()
    r_fwd, r_bwd, f_fwd, f_bwd = [], [], [], []
    for h in range(2):
        shared = pass_on(0, h, d_fwd[h])
        differentiate(h)
        r_fwd.append(line_sum(0, h, [(0, wdt, 0)], shared))
    for h in range(2):
        shared = pass_on(1, h, d_bwd[h])
        r_bwd.append(line_sum(1, h, [(1, wg, 1), (2, wu, 2)], shared))
    dg[...] = nt(all_rows(lambda h: gathered(h, core, 0)), all_rows(lambda h: whole(1, h))).astype(BF16)
    tokens = all_rows(lambda h: whole(0, h))
    for h in range(2):
        f_fwd += give_back(0, h, r_fwd[h])
    gg[...] = nt(tokens, all_rows(lambda h: gathered(h, core, 1))).astype(BF16)
    ug[...] = nt(tokens, all_rows(lambda h: gathered(h, core, 2))).astype(BF16)
    for h in range(2):
        f_bwd += give_back(1, h, r_bwd[h])
    for copy in f_fwd + f_bwd:
        copy.wait_recv()
    back[...] = f_dst[...]
    for copy in sends:
        copy.wait_send()


def finish(back, meta, gg, ug, dg, lo, ig, gg_h, ug_h, dg_h, sems):
    copies = [
        pltpu.make_async_copy(src, dst, sems.at[i]) for i, (src, dst) in enumerate([(gg, gg_h), (ug, ug_h), (dg, dg_h)])
    ]
    for copy in copies:
        copy.start()
    width, count = lo.shape
    sel = jnp.where(slot_numbers(count) == meta[0:1], 1.0, 0.0).astype(BF16)
    lo[...] = (meta[1:2] * nn(back[0, :, :, 0:width].reshape(NODES * CAP, width).T, sel)).astype(BF16)
    ig[...] = nn(back[1, :, :, 0:width].reshape(NODES * CAP, width).T, sel).astype(BF16)
    for copy in copies:
        copy.wait()


def on_device(tokens, out_grad, route_ids, route_weights, gate_weight, up_weight, down_weight):
    count, width = tokens.shape
    units, hid = gate_weight.shape[2], gate_weight.shape[3]
    slots = NODES * CAP
    run = slots // 2
    vmem = pl.BlockSpec(memory_space=pltpu.VMEM)
    hbm = pl.BlockSpec(memory_space=pltpu.HBM)
    dma = pltpu.SemaphoreType.DMA
    shapes = [
        ((128, count), BF16),
        ((128, count), BF16),
        (route_ids.shape[::-1], jnp.int32),
        (route_ids.shape[::-1], F32),
        ((2, 4, width, hid), BF16),
        ((2, 4, width, hid), BF16),
        ((hid, units), BF16),
        ((hid, units), BF16),
        ((hid, units), BF16),
        ((2, 4, width, hid), BF16),
        ((3, 4, width, hid), BF16),
        ((slots, count), BF16),
        ((2, NODES, CAP, 128), BF16),
        ((2, NODES, CAP, 128), BF16),
        ((2, 2, 2, 4, width, run), BF16),
        ((2, 4, 3, hid // 4, run), F32),
        ((2, 4, 3, hid // 4, run), BF16),
        ((2, 3, 3, hid // 4, run), BF16),
        ((2, 3, hid // 4, run), F32),
        ((2, 3, hid // 4, run), BF16),
        ((2, 3, hid // 4, run), BF16),
        ((2, 2, hid // 4, run), F32),
        ((2, 2, 4, 3, hid // 4, run), BF16),
        ((2, 2, 4, width, run), F32),
        ((2, 2, 4, width, run), BF16),
        ((2, 2, 3, width, run), BF16),
        ((2, NODES, CAP, 128), BF16),
        ((2, NODES, CAP, 128), BF16),
    ]
    sems = [(9,), (2, 7), (2, 7), (2, 2, 3), (2, 2, 3), (2, 2, 4), (2, 2, 4), (2, 2, 3), (2, 2, 3), (2, 2), (2, 2)]
    sems += [(2, 2, 3), (2, 2, 3), (2, 2, 4), (2, 2, 4), (2, 2, 3), (2, 2, 3), (2, 7), (2, 7), (3,), (3,)]
    operands = (
        tokens.T,
        out_grad.T,
        route_ids.T,
        route_weights.T,
        gate_weight.reshape(4, 2, width, hid),
        up_weight.reshape(4, 2, width, hid),
        down_weight.reshape(hid, units),
    )
    back, meta, gg, ug, dg = pl.pallas_call(
        kernel,
        out_shape=(
            jax.ShapeDtypeStruct((2, NODES, CAP, 128), BF16),
            jax.ShapeDtypeStruct((8, count), F32),
            jax.ShapeDtypeStruct((units, hid), BF16),
            jax.ShapeDtypeStruct((units, hid), BF16),
            jax.ShapeDtypeStruct((hid, units), BF16),
        ),
        in_specs=[hbm] * 7,
        out_specs=(vmem,) * 5,
        scratch_shapes=[pltpu.VMEM(shape, kind) for shape, kind in shapes] + [dma(shape) for shape in sems],
        compiler_params=pltpu.CompilerParams(collective_id=0, has_side_effects=True, vmem_limit_bytes=VMEM_BYTES),
        name="expert_layer",
    )(
        *(pltpu.with_memory_space_constraint(array, pltpu.HBM) for array in operands)
    )
    lo, ig, gg, ug, dg = pl.pallas_call(
        finish,
        out_shape=(
            jax.ShapeDtypeStruct((width, count), BF16),
            jax.ShapeDtypeStruct((width, count), BF16),
            jax.ShapeDtypeStruct((units, hid), BF16),
            jax.ShapeDtypeStruct((units, hid), BF16),
            jax.ShapeDtypeStruct((hid, units), BF16),
        ),
        in_specs=[vmem] * 5,
        out_specs=(vmem, vmem, hbm, hbm, hbm),
        scratch_shapes=[dma((3,))],
        compiler_params=pltpu.CompilerParams(vmem_limit_bytes=VMEM_BYTES),
        name="finish",
    )(back, meta, gg, ug, dg)
    return (lo.T, ig.T, gg[None, None], ug[None, None], dg[None, None])


def solution(mesh):
    rows = P("node", "local")
    routes = P("node", None)
    blocks = P("node", "local", None, None)
    return jax.shard_map(
        on_device,
        mesh=mesh,
        in_specs=(rows, rows, routes, routes, blocks, blocks, blocks),
        out_specs=(rows, rows, blocks, blocks, blocks),
        check_vma=False,
    )
```

time: 64.4 us -> 60.3 us (0.936)
  Pallas kernels: 63.3 us -> 59.5 us
    pallas_call x1, Pallas kernels: 61.5 us -> 57.7 us  [on_device(): pl.pallas_call(kernel, out_shape=(jax.ShapeDtypeStruct((2, NODES, CAP, 12...]
where the time goes in v3:
time: 60.3 us; the launch traced here: 60.1 us
  Pallas kernels  59.5 us (99%)
  between operations  0.64 us (1%)
    pallas_call x1, Pallas kernels, on_device(): pl.pallas_call(kernel, out_shape=(jax.ShapeDtypeStruct((2, NODES, CAP, 12...  57.7 us
    pallas_call x1, Pallas kernels, on_device(): pl.pallas_call(finish, out_shape=(jax.ShapeDtypeStruct((width, count), BF...  1.82 us

profile of v3, /device:TPU:1, one launch (start us, length us, event | category | flops | bytes accessed | tf_op | source)
XLA Modules:
  0.0 60.1 jit_solution(14567957021423094192)
XLA Ops:
  0.6 57.7 %expert_layer.1 = (bf16[2,8,32,128]{3,2,1,0:T(8,128)(2,1)S(1)}, f32[8,512]{1,0:T(8,128)S(1)}, bf16[896,256]{1,0:T(8,128)(2,1)S(1)}, bf16[896,256]{1,0:T(8,128)(2,1)S(1)}, bf16[256,896]{1,0:T(8,128)(2,1)S(1)}) custom-call(bf16[112,512]{1,0:T(8,128)(2,1)} %bitcast.15, bf16[112,512]{1,0:T(8,128)(2,1)} %bitcast.16, s32[8,512]{1,0:T(8,128)} %bitcast.17, ...), custom_call_target="tpu_custom_call" | custom-call | tf_op jit(solution)/shard_map/expert_layer/pallas_call | solution.py:376
  58.3 1.8 %finish.1 = (bf16[112,512]{1,0:T(8,128)(2,1)}, bf16[112,512]{1,0:T(8,128)(2,1)}, bf16[896,256]{1,0:T(8,128)(2,1)}, bf16[896,256]{1,0:T(8,128)(2,1)}, bf16[256,896]{1,0:T(8,128)(2,1)}) custom-call(bf16[2,8,32,128]{3,2,1,0:T(8,128)(2,1)S(1)} %get-tuple-element.15.back, f32[8,512]{1,0:T(8,128)S(1)} %get-tuple-element.16.meta, ...), custom_call_target="tpu_custom_call" | custom-call | tf_op jit(solution)/shard_map/finish/pallas_call | solution.py:393

commit v4 on v3

--- a/solution.py
+++ b/solution.py
@@ -32,7 +32,7 @@
 
 def kernel(
     tok_h, og_h, ids_h, wts_h, wg_h, wu_h, wd_h,
-    back, meta, gg, ug, dg,
+    lo, ig, gg, ug, dg,
     tok, og, ids, wts, wg, wu, wd, wgt, wut, wdt, far_w, sel, a_src, a_dst, held,
     c_own, c_src, c_dst, y_own, y_src, y_dst, act, rows, r_own, r_src, r_dst, f_src, f_dst,
     w_sem, as_sem, ar_sem, bs_sem, br_sem, gs_sem, gr_sem, cs_sem, cr_sem, ys_sem, yr_sem,
@@ -55,11 +55,12 @@
     z_peer = [{"node": (node + d) % NODES, "local": lane} for d in range(1, 8)]
     x_peer = [place((x + d) % 4, half, spot, core) for d in range(1, 4)]
     y_peer = [place(x, half, (spot + d) % 4, core) for d in range(1, 4)]
+    x_twin = [place((x + d) % 4, half, spot, 1 - core) for d in range(1, 4)]
     twin = place(x, half, spot, 1 - core)
     far = place(x, 1 - half, spot, core)
 
     barrier = pltpu.get_barrier_semaphore()
-    for peer in z_peer + x_peer + y_peer + [twin, far]:
+    for peer in z_peer + x_peer + x_twin + y_peer + [twin, far]:
         pl.semaphore_signal(barrier, inc=1, device_id=peer, device_id_type=MESH)
 
     sends = []
@@ -97,7 +98,7 @@
         load.start()
     tok[pl.ds(width, 128 - width)] = jnp.zeros((128 - width, count), BF16)
     og[pl.ds(width, 128 - width)] = jnp.zeros((128 - width, count), BF16)
-    before = lax.broadcasted_iota(jnp.int32, (count, count), 0) < lax.broadcasted_iota(jnp.int32, (count, count), 1)
+    before = lax.broadcasted_iota(jnp.int32, (128, 128), 0) < lax.broadcasted_iota(jnp.int32, (128, 128), 1)
     before = jnp.where(before, 1.0, 0.0).astype(BF16)
     loads[0].wait()
 
@@ -106,8 +107,13 @@
     owner = jnp.sum(jnp.where(match, ids[...] // (EXPERTS // NODES), 0), axis=0, keepdims=True)
     mine = (lax.broadcasted_iota(jnp.int32, (16, count), 0) == owner) & (hit > 0.0)
     mine = jnp.where(mine, 1.0, 0.0)
-    rank = nn(mine.astype(BF16), before)
-    rank = jnp.sum(mine * rank, axis=0, keepdims=True)
+    blocks = [mine[:, low : low + 128] for low in range(0, count, 128)]
+    within = nn(jnp.concatenate(blocks, axis=0).astype(BF16), before)
+    rank, passed = [], jnp.zeros((16, 1), F32)
+    for b, block in enumerate(blocks):
+        rank.append(jnp.sum(block * (within[16 * b : 16 * b + 16] + passed), axis=0, keepdims=True))
+        passed = passed + jnp.sum(block, axis=1, keepdims=True)
+    rank = jnp.concatenate(rank, axis=1)
     target = jnp.where(hit > 0.0, (owner * CAP).astype(F32) + rank, -1.0)
     sel[...] = jnp.where(slot_numbers(count) == target, 1.0, 0.0).astype(BF16)
 
@@ -187,14 +193,17 @@
         block = rows.at[h, core, x, span]
         out = [send(block, block, ds_sem.at[s, h, d - 1], dr_sem.at[s, h, d - 1], x_peer[d - 1]) for d in range(1, 4)]
         shared = [send(block, block, es_sem.at[s, h, 0], er_sem.at[s, h, 0], twin)]
+        if s == 0:
+            shared += [send(block, block, es_sem.at[s, h, d], er_sem.at[s, h, d], x_twin[d - 1]) for d in range(1, 4)]
         return span, out, shared
 
     def pass_on(s, h, state):
         span, out, shared = state
         for d in range(1, 4):
             out[d - 1].wait_recv()
-            block = rows.at[h, core, (x + 4 - d) % 4, span]
-            shared.append(send(block, block, es_sem.at[s, h, d], er_sem.at[s, h, d], twin))
+            if s == 1:
+                block = rows.at[h, core, (x + 4 - d) % 4, span]
+                shared.append(send(block, block, es_sem.at[s, h, d], er_sem.at[s, h, d], twin))
         return shared
 
     def gathered(h, which, i):
@@ -234,15 +243,13 @@
             f_dst[s, node] = f_src[s, 0]
         return out
 
-    pl.semaphore_wait(barrier, 15)
+    pl.semaphore_wait(barrier, 18)
     loads[2].wait()
     a_tok = dispatch(0, tok[...])
     loads[1].wait()
     share = jnp.sum(jnp.where(match, wts[...], 0.0), axis=0, keepdims=True)
     loads[3].wait()
     a_grad = dispatch(1, (share * og[...].astype(F32)).astype(BF16))
-    meta[0:1] = target
-    meta[1:2] = share
 
     for load in loads[4:]:
         load.wait()
@@ -303,23 +310,23 @@
     ug[...] = nt(tokens, all_rows(lambda h: gathered(h, core, 2))).astype(BF16)
     for h in range(2):
         f_bwd += give_back(1, h, r_bwd[h])
-    for copy in f_fwd + f_bwd:
-        copy.wait_recv()
-    back[...] = f_dst[...]
+
+    def combine(s, copies):
+        for copy in copies:
+            copy.wait_recv()
+        return nn(f_dst[s, :, :, 0:width].reshape(slots, width).T, sel[...])
+
+    lo[...] = (share * combine(0, f_fwd)).astype(BF16)
+    ig[...] = combine(1, f_bwd).astype(BF16)
     for copy in sends:
         copy.wait_send()
 
 
-def finish(back, meta, gg, ug, dg, lo, ig, gg_h, ug_h, dg_h, sems):
-    copies = [
-        pltpu.make_async_copy(src, dst, sems.at[i]) for i, (src, dst) in enumerate([(gg, gg_h), (ug, ug_h), (dg, dg_h)])
-    ]
+def finish(*refs):
+    count = len(refs) // 2
+    copies = [pltpu.make_async_copy(refs[i], refs[count + i], refs[-1].at[i]) for i in range(count)]
     for copy in copies:
         copy.start()
-    width, count = lo.shape
-    sel = jnp.where(slot_numbers(count) == meta[0:1], 1.0, 0.0).astype(BF16)
-    lo[...] = (meta[1:2] * nn(back[0, :, :, 0:width].reshape(NODES * CAP, width).T, sel)).astype(BF16)
-    ig[...] = nn(back[1, :, :, 0:width].reshape(NODES * CAP, width).T, sel).astype(BF16)
     for copy in copies:
         copy.wait()
 
@@ -373,11 +380,11 @@
         up_weight.reshape(4, 2, width, hid),
         down_weight.reshape(hid, units),
     )
-    back, meta, gg, ug, dg = pl.pallas_call(
+    results = pl.pallas_call(
         kernel,
         out_shape=(
-            jax.ShapeDtypeStruct((2, NODES, CAP, 128), BF16),
-            jax.ShapeDtypeStruct((8, count), F32),
+            jax.ShapeDtypeStruct((width, count), BF16),
+            jax.ShapeDtypeStruct((width, count), BF16),
             jax.ShapeDtypeStruct((units, hid), BF16),
             jax.ShapeDtypeStruct((units, hid), BF16),
             jax.ShapeDtypeStruct((hid, units), BF16),
@@ -400,11 +407,11 @@
             jax.ShapeDtypeStruct((hid, units), BF16),
         ),
         in_specs=[vmem] * 5,
-        out_specs=(vmem, vmem, hbm, hbm, hbm),
-        scratch_shapes=[dma((3,))],
+        out_specs=(hbm,) * 5,
+        scratch_shapes=[dma((5,))],
         compiler_params=pltpu.CompilerParams(vmem_limit_bytes=VMEM_BYTES),
         name="finish",
-    )(back, meta, gg, ug, dg)
+    )(*results)
     return (lo.T, ig.T, gg[None, None], ug[None, None], dg[None, None])
 
 

time: 60.3 us -> 59.8 us (level)
    pallas_call x1, Pallas kernels: 1.82 us -> 1.19 us  [on_device(): pl.pallas_call(finish, out_shape=(jax.ShapeDtypeStruct((width, count), BF...]
where the time goes in v4:
time: 59.8 us; the launch traced here: 59.6 us
  Pallas kernels  59 us (99%)
  between operations  0.64 us (1%)
    pallas_call x1, Pallas kernels, on_device(): pl.pallas_call(kernel, out_shape=(jax.ShapeDtypeStruct((width, count), BF...  57.8 us

profile of v4, /device:TPU:1, one launch (start us, length us, event | category | flops | bytes accessed | tf_op | source)
XLA Modules:
  0.0 59.6 jit_solution(14911993756225432191)
XLA Ops:
  0.6 57.8 %expert_layer.1 = (bf16[112,512]{1,0:T(8,128)(2,1)S(1)}, bf16[112,512]{1,0:T(8,128)(2,1)S(1)}, bf16[896,256]{1,0:T(8,128)(2,1)S(1)}, bf16[896,256]{1,0:T(8,128)(2,1)S(1)}, bf16[256,896]{1,0:T(8,128)(2,1)S(1)}) custom-call(bf16[112,512]{1,0:T(8,128)(2,1)} %bitcast.15, bf16[112,512]{1,0:T(8,128)(2,1)} %bitcast.16, s32[8,512]{1,0:T(8,128)} %bitcast.17, ...), custom_call_target="tpu_custom_call" | custom-call | tf_op jit(solution)/shard_map/expert_layer/pallas_call | solution.py:383
  58.5 1.2 %finish.1 = (bf16[112,512]{1,0:T(8,128)(2,1)}, bf16[112,512]{1,0:T(8,128)(2,1)}, bf16[896,256]{1,0:T(8,128)(2,1)}, bf16[896,256]{1,0:T(8,128)(2,1)}, bf16[256,896]{1,0:T(8,128)(2,1)}) custom-call(bf16[112,512]{1,0:T(8,128)(2,1)S(1)} %get-tuple-element.15.refs_0_, bf16[112,512]{1,0:T(8,128)(2,1)S(1)} %get-tuple-element.16.refs_1_, ...), custom_call_target="tpu_custom_call" | custom-call | tf_op jit(solution)/shard_map/finish/pallas_call | solution.py:400

commit v5 on v4

--- a/solution.py
+++ b/solution.py
@@ -236,7 +236,7 @@
             total = total + r_dst[s, h, d - 1].astype(F32)
         f_src[s, low:high, :, 0:width] = total.astype(BF16).T.reshape(high - low, CAP, width)
         out = []
-        for j in range(max(low, 1), high):
+        for j in reversed(range(max(low, 1), high)):
             peer = {"node": after(j), "local": lane}
             out.append(send(f_src.at[s, j], f_dst.at[s, node], fs_sem.at[s, j - 1], fr_sem.at[s, j - 1], peer))
         if low == 0:

time: 59.8 us -> 59.8 us (level)
  no operation moved by 1% of the time
where the time goes in v5:
time: 59.8 us; the launch traced here: 59.7 us
  Pallas kernels  59 us (99%)
  between operations  0.64 us (1%)
    pallas_call x1, Pallas kernels, on_device(): pl.pallas_call(kernel, out_shape=(jax.ShapeDtypeStruct((width, count), BF...  57.8 us

profile of v5, /device:TPU:1, one launch (start us, length us, event | category | flops | bytes accessed | tf_op | source)
XLA Modules:
  0.0 59.7 jit_solution(7950464512979669733)
XLA Ops:
  0.6 57.8 %expert_layer.1 = (bf16[112,512]{1,0:T(8,128)(2,1)S(1)}, bf16[112,512]{1,0:T(8,128)(2,1)S(1)}, bf16[896,256]{1,0:T(8,128)(2,1)S(1)}, bf16[896,256]{1,0:T(8,128)(2,1)S(1)}, bf16[256,896]{1,0:T(8,128)(2,1)S(1)}) custom-call(bf16[112,512]{1,0:T(8,128)(2,1)} %bitcast.15, bf16[112,512]{1,0:T(8,128)(2,1)} %bitcast.16, s32[8,512]{1,0:T(8,128)} %bitcast.17, ...), custom_call_target="tpu_custom_call" | custom-call | tf_op jit(solution)/shard_map/expert_layer/pallas_call | solution.py:383
  58.5 1.2 %finish.1 = (bf16[112,512]{1,0:T(8,128)(2,1)}, bf16[112,512]{1,0:T(8,128)(2,1)}, bf16[896,256]{1,0:T(8,128)(2,1)}, bf16[896,256]{1,0:T(8,128)(2,1)}, bf16[256,896]{1,0:T(8,128)(2,1)}) custom-call(bf16[112,512]{1,0:T(8,128)(2,1)S(1)} %get-tuple-element.15.refs_0_, bf16[112,512]{1,0:T(8,128)(2,1)S(1)} %get-tuple-element.16.refs_1_, ...), custom_call_target="tpu_custom_call" | custom-call | tf_op jit(solution)/shard_map/finish/pallas_call | solution.py:400
